TPU v7x, 32 devices: a whole 2x2x4 slice. The times are simulated.
32 devices in a mesh: ctx: 8 (over z, y), kv: 4 (over x, core).
Axes of the slice: x: 2, y: 2, z: 4, core: 2. Of those that a mesh axis runs over, the one named last changes fastest.
Arguments:
- tokens: bfloat16 [4096, 8192], P('ctx', 'kv'), may hold values from -6 to 6
- segment_ids: int32 [4096], replicated, may hold values from 0 to 15, never falling along the last dimension, each value on 1 to 1024 neighbouring positions
- query_weight: bfloat16 [8192, 4096], P('ctx', 'kv'), may hold values from -2 to 2
- key_weight: bfloat16 [8192, 512], P('ctx', 'kv'), may hold values from -2 to 2
- value_projection_matrix: bfloat16 [8192, 512], P('ctx', 'kv'), may hold values from -0.0625 to 0.0625
Outputs:
- attended: bfloat16 [4096, 4096], P('ctx', 'kv')
Inputs may be any that keep to these rules, and one draw needn't show every extreme that they name: `segment_ids`: segment ids never fall along the sequence; each document holds 1 to 1024 tokens and one holds exactly 1024.
All inputs are finite; a program needn't handle non-finite values.
Results may differ from a plain program's by a relative error of at most 0.0085.
Values may be sent and summed in bfloat16 or wider, within the bound.
A program may use at most 128 MiB of HBM per device.

v0:
```python
import jax
import jax.numpy as jnp
from jax import lax
from jax.sharding import PartitionSpec as P

HEAD_DIMENSION = 128


def shifted(shard, axis, by):
    length = lax.axis_size(axis)
    pairs = [(i, i + by) for i in range(length) if 0 <= i + by < length]
    return lax.ppermute(shard, axis, pairs)


def attend_block(query_matrix, key_matrix, value_matrix, visible):
    head_size = query_matrix.shape[-1]
    scores = jnp.einsum(
        "thgd,shd->hgts", query_matrix, key_matrix, preferred_element_type=jnp.float32
    ) * head_size ** (-0.5)
    scores = jnp.where(visible[None, None], scores, -1e30)
    largest = jnp.max(scores, axis=-1, keepdims=True)
    expon = jnp.where(visible[None, None], jnp.exp(scores - largest), 0.0)
    total = jnp.sum(expon, axis=-1, keepdims=True)
    weights = expon.astype(jnp.bfloat16)
    summed = jnp.einsum("hgts,shd->hgtd", weights, value_matrix, preferred_element_type=jnp.float32)
    result = summed / total
    rows = query_matrix.shape[0]
    return jnp.transpose(result, (2, 0, 1, 3)).reshape(rows, -1).astype(jnp.bfloat16)


def shards(tokens, segment_ids, query_weight, key_weight, value_projection_matrix):
    whole = lax.all_gather(tokens, "kv", axis=1, tiled=True)
    rows = whole.shape[0]

    def add_rows(piece):
        return jnp.dot(whole, piece, preferred_element_type=jnp.float32)

    q_sum = add_rows(lax.all_gather(query_weight, "ctx", axis=0, tiled=True))
    k_sum = add_rows(lax.all_gather(key_weight, "ctx", axis=0, tiled=True))
    v_sum = add_rows(lax.all_gather(value_projection_matrix, "ctx", axis=0, tiled=True))
    query_rows = q_sum.astype(jnp.bfloat16)
    key_rows = k_sum.astype(jnp.bfloat16)
    value_rows = v_sum.astype(jnp.bfloat16)
    prev_key, prev_value = shifted((key_rows, value_rows), "ctx", 1)
    kv_heads = key_weight.shape[1] // HEAD_DIMENSION
    query_group = query_weight.shape[1] // (HEAD_DIMENSION * kv_heads)
    query_matrix = query_rows.reshape(rows, kv_heads, query_group, HEAD_DIMENSION)
    nearby_keys = jnp.concatenate([prev_key, key_rows], axis=0).reshape(
        2 * rows, kv_heads, HEAD_DIMENSION
    )
    nearby_values = jnp.concatenate([prev_value, value_rows], axis=0).reshape(
        2 * rows, kv_heads, HEAD_DIMENSION
    )
    position = lax.axis_index("ctx")
    begin_offset = position * rows
    prev_start = jnp.maximum(begin_offset - rows, 0)
    seg_query = lax.dynamic_slice_in_dim(segment_ids, begin_offset, rows, 0)
    seg_prev = lax.dynamic_slice_in_dim(segment_ids, prev_start, rows, 0)
    seg_keys = jnp.concatenate([seg_prev, seg_query], axis=0)
    qpos = begin_offset + jnp.arange(rows, dtype=jnp.int32)
    kpos = begin_offset - rows + jnp.arange(2 * rows, dtype=jnp.int32)
    visible = (kpos[None, :] <= qpos[:, None]) & (kpos[None, :] > qpos[:, None] - rows)
    visible = visible & (kpos[None, :] >= 0) & (seg_keys[None, :] == seg_query[:, None])
    return attend_block(query_matrix, nearby_keys, nearby_values, visible)


def solution(mesh):
    placed = (P("ctx", "kv"), P(), P("ctx", "kv"), P("ctx", "kv"), P("ctx", "kv"))
    return jax.shard_map(
        shards, mesh=mesh, in_specs=placed, out_specs=P("ctx", "kv"), check_vma=False
    )
```

profile of v0, /device:TPU:0, one launch (start us, length us, event | category | flops | bytes accessed | tf_op | source)
XLA Modules:
  0.0 434.3 jit_solution(8953648349559909561)
XLA Ops:
  6.5 0.0 all-gather.11.cloned.1.call-start
  6.5 0.7 all-gather.11.cloned.1.call-update
  7.3 0.0 all-gather.5.cloned.1.call-start
  7.3 0.7 all-gather.5.cloned.1.call-update
  8.0 0.0 all-gather.7.cloned.1.call-start
  8.1 0.7 all-gather.7.cloned.1.call-update
  8.7 0.0 all-gather.9.cloned.1.call-start
  8.8 0.5 all-gather.9.cloned.1.call-update
  9.3 0.8 fusion.22
  10.2 1.0 compare_and_fusion
  11.2 50.3 %all-gather.11.cloned.1.call-done = bf16[8192,128]{1,0:T(8,128)(2,1)} async-done(((bf16[1024,128]{1,0:T(8,128)(2,1)}), bf16[8192,128]{1,0:T(8,128)(2,1)}) %all-gather.11.cloned.1.call-update) | async-done | bytes 2097168 | tf_op jit(solution)/shard_map/all_gather | solution.py:40
  61.5 58.4 %all-gather.5.cloned.1.call-done = bf16[512,8192]{1,0:T(8,128)(2,1)} async-done(((bf16[512,2048]{1,0:T(8,128)(2,1)}), bf16[512,8192]{1,0:T(8,128)(2,1)}) %all-gather.5.cloned.1.call-update) | async-done | bytes 8388624 | tf_op jit(solution)/shard_map/all_gather | solution.py:32
  119.9 6.3 %convolution_convert_fusion.1 = bf16[512,128]{1,0:T(8,128)(2,1)S(1)} fusion(bf16[512,8192]{1,0:T(8,128)(2,1)} %all-gather.5.cloned.1.call-done, bf16[8192,128]{1,0:T(8,128)(2,1)} %all-gather.11.cloned.1.call-done), kind=kOutput, calls=%fused_computation.12 | convolution fusion | flops 1073807360 | bytes 10616832 | tf_op jit(solution)/shard_map/dot_general | solution.py:36
  126.2 3.4 collective-permute-start.1
  129.6 42.6 %all-gather.7.cloned.1.call-done = bf16[8192,128]{1,0:T(8,128)(2,1)} async-done(((bf16[1024,128]{1,0:T(8,128)(2,1)}), bf16[8192,128]{1,0:T(8,128)(2,1)}) %all-gather.7.cloned.1.call-update) | async-done | bytes 2097168 | tf_op jit(solution)/shard_map/all_gather | solution.py:39
  172.2 6.3 %convolution_convert_fusion.2 = bf16[512,128]{1,0:T(8,128)(2,1)S(1)} fusion(bf16[512,8192]{1,0:T(8,128)(2,1)} %all-gather.5.cloned.1.call-done, bf16[8192,128]{1,0:T(8,128)(2,1)} %all-gather.7.cloned.1.call-done), kind=kOutput, calls=%fused_computation.13 | convolution fusion | flops 1073807360 | bytes 10616832 | tf_op jit(solution)/shard_map/dot_general | solution.py:36
  178.5 2.6 collective-permute-start
  181.1 219.3 %all-gather.9.cloned.1.call-done = bf16[8192,1024]{1,0:T(8,128)(2,1)} async-done(((bf16[1024,1024]{1,0:T(8,128)(2,1)}), bf16[8192,1024]{1,0:T(8,128)(2,1)}) %all-gather.9.cloned.1.call-update) | async-done | bytes 16777232 | tf_op jit(solution)/shard_map/all_gather | solution.py:38
  400.4 14.8 %fusion.7 = bf16[64,8,8,128]{3,2,1,0:T(8,128)(2,1)S(1)} fusion(bf16[512,8192]{1,0:T(8,128)(2,1)} %all-gather.5.cloned.1.call-done, bf16[8192,1024]{1,0:T(8,128)(2,1)} %all-gather.9.cloned.1.call-done), kind=kOutput, calls=%fused_computation.11 | convolution fusion | flops 8590458880 | bytes 26214400 | tf_op jit(solution)/shard_map/dot_general | solution.py:36
  415.1 0.0 collective-permute-done
  415.2 2.9 fusion
  418.1 4.0 fusion.1
  422.1 0.0 collective-permute-done.1
  422.1 4.3 divide_convert_fusion
  426.4 1.3 copy.9
  (3 shorter events, 0.0 us)
Async XLA Ops:
  6.5 55.0 %all-gather.11.cloned.1.call-start = ((), (), s32[]{:S(2)}) async-start(), calls=%async_computation.3 | async-start | bytes 2359296 | tf_op jit(solution)/shard_map/all_gather | solution.py:40
  7.3 112.6 %all-gather.5.cloned.1.call-start = ((), (), s32[]{:S(2)}) async-start(), calls=%async_computation | async-start | bytes 10485760 | tf_op jit(solution)/shard_map/all_gather | solution.py:32
  8.0 164.1 %all-gather.7.cloned.1.call-start = ((), (), s32[]{:S(2)}) async-start(), calls=%async_computation.1 | async-start | bytes 2359296 | tf_op jit(solution)/shard_map/all_gather | solution.py:39
  8.7 391.6 %all-gather.9.cloned.1.call-start = ((), (), s32[]{:S(2)}) async-start(), calls=%async_computation.2 | async-start | bytes 18874368 | tf_op jit(solution)/shard_map/all_gather | solution.py:38
  126.2 295.9 %collective-permute-start.1 = (bf16[512,128]{1,0:T(8,128)(2,1)S(1)}, bf16[512,128]{1,0:T(8,128)(2,1)S(1)}, u32[]{:S(2)}, u32[]{:S(2)}) collective-permute-start(bf16[512,128]{1,0:T(8,128)(2,1)S(1)} %convolution_convert_fusion.1), channel_id=1, source_target_pairs={{0,4},{4,8},{8,12},{12,16},{16,20},{20,24},{24,28},{1,5},{5,9},{9,... | collective-permute-start | bytes 393224 | tf_op jit(solution)/shard_map/ppermute | solution.py:12
  178.5 236.7 %collective-permute-start = (bf16[512,128]{1,0:T(8,128)(2,1)S(1)}, bf16[512,128]{1,0:T(8,128)(2,1)S(1)}, u32[]{:S(2)}, u32[]{:S(2)}) collective-permute-start(bf16[512,128]{1,0:T(8,128)(2,1)S(1)} %convolution_convert_fusion.2), channel_id=1, source_target_pairs={{0,4},{4,8},{8,12},{12,16},{16,20},{20,24},{24,28},{1,5},{5,9},{9,... | collective-permute-start | bytes 393224 | tf_op jit(solution)/shard_map/ppermute | solution.py:12
Sparse Core Ops, SparseCore 0:
  9.5 51.9 all-gather.10
  63.1 56.7 all-gather.4
  122.0 50.1 all-gather.6
  174.1 226.1 all-gather.8
where the time goes:
time: 435 us; the launch traced here: 434 us
  waiting for transfers between devices  373 us (86%)
  matrix products  34.6 us (8%)
  between operations  13.2 us (3%)
  starting transfers between devices  6.15 us (1%)
  other arithmetic  5.01 us (1%)
    all_gather x1, waiting for transfers between devices, shards(): q_sum = add_rows(lax.all_gather(query_weight, 'ctx', axis=0, tiled=True))  219 us
    all_gather x1, waiting for transfers between devices, shards(): whole = lax.all_gather(tokens, 'kv', axis=1, tiled=True)  58.4 us
    all_gather x1, waiting for transfers between devices, shards(): lax.all_gather(value_projection_matrix, 'ctx', axis=0, tiled=True)  50.3 us
    all_gather x1, waiting for transfers between devices, shards(): k_sum = add_rows(lax.all_gather(key_weight, 'ctx', axis=0, tiled=True))  42.6 us
    dot_general x3, matrix products, add_rows(): return jnp.dot(whole, piece, preferred_element_type=jnp.float32)  27.4 us
  transfers between devices with their start and end apart: 6, of which 4 were waited for; matrix products, arithmetic and copies ran while one was open for 8% of the time, Pallas kernels for 0%

commit v1 on v0

--- a/solution.py
+++ b/solution.py
@@ -1,6 +1,10 @@
+import functools
+
 import jax
 import jax.numpy as jnp
 from jax import lax
+from jax.experimental import pallas as pl
+from jax.experimental.pallas import tpu as pltpu
 from jax.sharding import PartitionSpec as P
 
 HEAD_DIMENSION = 128
@@ -28,19 +32,141 @@
     return jnp.transpose(result, (2, 0, 1, 3)).reshape(rows, -1).astype(jnp.bfloat16)
 
 
+MESH = pl.DeviceIdType.MESH
+
+
+def gather_kernel(lines, pieces, tok, wgt, tok_all, wgt_all, loc, tsend, trecv,
+                  up_s, up_r, dn_s, dn_r, y_s, y_r):
+    ctx, kv = lax.axis_index("ctx"), lax.axis_index("kv")
+    z, y = ctx // 2, ctx % 2
+    up, down, across = {"ctx": ctx + 2}, {"ctx": ctx - 2}, {"ctx": z * 2 + (1 - y)}
+    core = {"kv": (kv // 2) * 2 + (1 - kv % 2)}
+    far = {"kv": (1 - kv // 2) * 2 + kv % 2}
+    has_up, has_down = z < lines - 1, z > 0
+    height, depth = tok.shape[1], wgt.shape[0]
+    rows = depth // pieces
+
+    barrier = pltpu.get_barrier_semaphore()
+    for other in (across, core, far):
+        pl.semaphore_signal(barrier, inc=1, device_id=other, device_id_type=MESH)
+
+    @pl.when(has_up)
+    def _():
+        pl.semaphore_signal(barrier, inc=1, device_id=up, device_id_type=MESH)
+
+    @pl.when(has_down)
+    def _():
+        pl.semaphore_signal(barrier, inc=1, device_id=down, device_id_type=MESH)
+
+    pl.semaphore_wait(barrier, 3 + has_up.astype(jnp.int32) + has_down.astype(jnp.int32))
+
+    def copy(src, dst, send, recv, other):
+        return pltpu.make_async_remote_copy(
+            src_ref=src, dst_ref=dst, send_sem=send, recv_sem=recv,
+            device_id=other, device_id_type=MESH)
+
+    def place(line, side, p):
+        start = pl.multiple_of((line * 2 + side) * depth + p * rows, rows)
+        return wgt_all.at[pl.ds(start, rows), :]
+
+    def block(off, p):
+        return wgt.at[pl.ds(p * rows, rows), :] if off == 0 else place(z + off, y, p)
+
+    def up_copy(d, p):
+        return copy(block(-d, p), place(z - d, y, p), up_s.at[d, p], up_r.at[d, p], up)
+
+    def down_copy(d, p):
+        return copy(block(d, p), place(z + d, y, p), dn_s.at[d, p], dn_r.at[d, p], down)
+
+    def y_copy(off, p):
+        i = off + lines - 1
+        return copy(block(off, p), place(z + off, y, p), y_s.at[i, p], y_r.at[i, p], across)
+
+    def columns(k):
+        return tok_all.at[:, pl.ds(pl.multiple_of(k * height, height), height)]
+
+    for p in range(pieces):
+        pl.when(has_up)(lambda p=p: up_copy(0, p).start())
+        pl.when(has_down)(lambda p=p: down_copy(0, p).start())
+        y_copy(0, p).start()
+    other_core = core["kv"]
+    own_far = copy(tok, columns(kv), tsend.at[0], trecv.at[0], far)
+    own_core = copy(tok, columns(kv), tsend.at[1], trecv.at[1], core)
+    pass_on = copy(columns(far["kv"]), columns(far["kv"]), tsend.at[2], trecv.at[2], core)
+    own_far.start()
+    own_core.start()
+    local = [pltpu.make_async_copy(tok, columns(kv), loc.at[0]),
+             pltpu.make_async_copy(
+                 wgt, wgt_all.at[pl.ds(pl.multiple_of(ctx * depth, depth), depth), :], loc.at[1])]
+    for c in local:
+        c.start()
+
+    for d in range(1, lines):
+        for p in range(pieces):
+            @pl.when(z >= d)
+            def _(d=d, p=p):
+                up_copy(d - 1, p).wait_recv()
+                y_copy(-d, p).start()
+                if d < lines - 1:
+                    pl.when(has_up)(lambda: up_copy(d, p).start())
+
+            @pl.when(z + d < lines)
+            def _(d=d, p=p):
+                down_copy(d - 1, p).wait_recv()
+                y_copy(d, p).start()
+                if d < lines - 1:
+                    pl.when(has_down)(lambda: down_copy(d, p).start())
+        if d == 1:
+            own_far.wait_recv()
+            pass_on.start()
+    if lines == 1:
+        own_far.wait_recv()
+        pass_on.start()
+
+    own_core.wait_recv()
+    pass_on.wait_recv()
+    for c in (own_far, own_core, pass_on):
+        c.wait_send()
+    for c in local:
+        c.wait()
+    for p in range(pieces):
+        for d in range(lines):
+            if d < lines - 1:
+                pl.when(has_up & (z >= d))(lambda d=d, p=p: up_copy(d, p).wait_send())
+                pl.when(has_down & (z + d < lines))(lambda d=d, p=p: down_copy(d, p).wait_send())
+            pl.when(z >= d)(lambda d=d, p=p: y_copy(-d, p).wait())
+            if d > 0:
+                pl.when(z + d < lines)(lambda d=d, p=p: y_copy(d, p).wait())
+
+
+def gathered(tokens, weights):
+    lines = lax.axis_size("ctx") // 2
+    depth, width = weights.shape
+    pieces = max(1, depth // 256)
+    dma = pltpu.SemaphoreType.DMA
+    line_sems = [dma((lines, pieces))] * 4
+    return pl.pallas_call(
+        functools.partial(gather_kernel, lines, pieces),
+        out_shape=(
+            jax.ShapeDtypeStruct((tokens.shape[0], tokens.shape[1] * lax.axis_size("kv")), tokens.dtype),
+            jax.ShapeDtypeStruct((depth * lax.axis_size("ctx"), width), weights.dtype),
+        ),
+        in_specs=[pl.BlockSpec(memory_space=pl.ANY)] * 2,
+        out_specs=[pl.BlockSpec(memory_space=pl.ANY)] * 2,
+        scratch_shapes=[dma((2,)), dma((3,)), dma((3,))] + line_sems
+        + [dma((2 * lines - 1, pieces))] * 2,
+        compiler_params=pltpu.CompilerParams(collective_id=0, has_side_effects=True),
+    )(tokens, weights)
+
+
 def shards(tokens, segment_ids, query_weight, key_weight, value_projection_matrix):
-    whole = lax.all_gather(tokens, "kv", axis=1, tiled=True)
-    rows = whole.shape[0]
-
-    def add_rows(piece):
-        return jnp.dot(whole, piece, preferred_element_type=jnp.float32)
-
-    q_sum = add_rows(lax.all_gather(query_weight, "ctx", axis=0, tiled=True))
-    k_sum = add_rows(lax.all_gather(key_weight, "ctx", axis=0, tiled=True))
-    v_sum = add_rows(lax.all_gather(value_projection_matrix, "ctx", axis=0, tiled=True))
-    query_rows = q_sum.astype(jnp.bfloat16)
-    key_rows = k_sum.astype(jnp.bfloat16)
-    value_rows = v_sum.astype(jnp.bfloat16)
+    rows = tokens.shape[0]
+    packed = jnp.concatenate([key_weight, value_projection_matrix, query_weight], axis=1)
+    whole, weights = gathered(tokens, packed)
+    wide = key_weight.shape[1]
+    key_value = jnp.dot(whole, weights[:, :2 * wide], preferred_element_type=jnp.float32).astype(jnp.bfloat16)
+    key_rows, value_rows = key_value[:, :wide], key_value[:, wide:]
+    query_rows = jnp.dot(whole, weights[:, 2 * wide:], preferred_element_type=jnp.float32).astype(jnp.bfloat16)
     prev_key, prev_value = shifted((key_rows, value_rows), "ctx", 1)
     kv_heads = key_weight.shape[1] // HEAD_DIMENSION
     query_group = query_weight.shape[1] // (HEAD_DIMENSION * kv_heads)

time: 435 us -> 278 us (0.64)
  waiting for transfers between devices: 373 us -> 0.01 us
  Pallas kernels: 0 us -> 231 us
  between operations: 13.2 us -> 0.12 us
  matrix products: 34.6 us -> 29 us
    all_gather x4 -> x0, waiting for transfers between devices: 371 us -> none  [the longest x1 219 us: shards(): q_sum = add_rows(lax.all_gather(query_weight, 'ctx', axis=0, tiled=True))]
    pallas_call x0 -> x1, Pallas kernels: none -> 231 us  [gathered(): pl.pallas_call(functools.partial(gather_kernel, lines, pieces), out_shape...]
    dot_general x3 -> x2, matrix products: 27.4 us -> 21.8 us  [the longest x1 14.8 us: shards(): jnp.dot(whole, weights[:, 2 * wide:], preferred_element_type=jnp.float32)]
  transfers between devices with their start and end apart: 6 -> 2, of which waited for: 4 -> 0; matrix products, arithmetic and copies ran while one was open for 8% -> 8% of each run, Pallas kernels for 0% -> 0%
where the time goes in v1:
time: 278 us
  Pallas kernels  231 us (83%)
  matrix products  29 us (10%)
  other arithmetic  8.38 us (3%)
  starting transfers between devices  7.07 us (3%)
    pallas_call x1, Pallas kernels, gathered(): pl.pallas_call(functools.partial(gather_kernel, lines, pieces), out_shape...  231 us
    dot_general x1, matrix products, shards(): jnp.dot(whole, weights[:, 2 * wide:], preferred_element_type=jnp.float32)  14.8 us
    ppermute x2, starting transfers between devices, shifted(): return lax.ppermute(shard, axis, pairs)  7.07 us
    dot_general x1, matrix products, shards(): jnp.dot(whole, weights[:, :2 * wide], preferred_element_type=jnp.float32)  6.97 us
  transfers between devices with their start and end apart: 2, of which 0 were waited for; matrix products, arithmetic and copies ran while one was open for 8% of the time, Pallas kernels for 0%

profile of v1, /device:TPU:0, one launch (start us, length us, event | category | flops | bytes accessed | tf_op | source)
XLA Modules:
  0.0 277.9 jit_solution(5318136366794307333)
XLA Ops:
  0.0 3.4 %pad_maximum_fusion.wgt = bf16[1024,1280]{1,0:T(8,128)(2,1)} fusion(bf16[1024,1024]{1,0:T(8,128)(2,1)} %param.7, bf16[1024,128]{1,0:T(8,128)(2,1)} %param.9, bf16[1024,128]{1,0:T(8,128)(2,1)} %param.8), kind=kLoop, calls=%fused_computation.12 | loop fusion | flops 7864320 | bytes 5242880 | tf_op jit(solution)/shard_map/concatenate | solution.py:164
  3.4 231.2 %shard_map.55 = (bf16[512,8192]{1,0:T(8,128)(2,1)}, bf16[8192,1280]{1,0:T(8,128)(2,1)}) custom-call(bf16[512,2048]{1,0:T(8,128)(2,1)} %tok.1, bf16[1024,1280]{1,0:T(8,128)(2,1)} %pad_maximum_fusion.wgt), custom_call_target="tpu_custom_call" | custom-call | tf_op jit(solution)/shard_map/pallas_call | solution.py:148
  234.5 7.0 %fusion.17 = bf16[512,256]{1,0:T(8,128)(2,1)S(1)} fusion(bf16[512,8192]{1,0:T(8,128)(2,1)} %get-tuple-element.7, bf16[8192,1280]{1,0:T(8,128)(2,1)} %get-tuple-element.8), kind=kOutput, calls=%fused_computation.17 | convolution fusion | flops 2147614720 | bytes 12845056 | tf_op jit(solution)/shard_map/dot_general | solution.py:167
  241.5 2.4 collective-permute-start.1
  244.0 4.7 %collective-permute-start = (bf16[512,128]{1,0:T(8,128)(2,1)S(1)}, bf16[512,128]{1,0:T(8,128)(2,1)S(1)}, u32[]{:S(2)}, u32[]{:S(2)}) collective-permute-start(bf16[512,128]{1,0:T(8,128)(2,1)S(1)} %get-tuple-element.10), channel_id=1, source_target_pairs={{0,4},{4,8},{8,12},{12,16},{16,20},{20,24},{24,28},{1,5},{5,9},{9,... | collective-permute-start | bytes 393224 | tf_op jit(solution)/shard_map/ppermute | solution.py:16
  248.7 14.8 %fusion.14 = bf16[64,8,8,128]{3,2,1,0:T(8,128)(2,1)S(1)} fusion(bf16[512,8192]{1,0:T(8,128)(2,1)} %get-tuple-element.7, bf16[8192,1280]{1,0:T(8,128)(2,1)} %get-tuple-element.8), kind=kOutput, calls=%fused_computation.16 | convolution fusion | flops 8590458880 | bytes 26214400 | tf_op jit(solution)/shard_map/dot_general | solution.py:169
  263.5 0.8 fusion.35
  264.3 1.0 compare_and_fusion
  265.3 0.0 collective-permute-done
  265.3 2.9 %fusion.2 = (f32[8,512]{1,0:T(8,128)S(1)}, f32[1024,512,8]{1,0,2:T(8,128)S(1)}) fusion(pred[512,1024]{0,1:T(8,128)(4,1)S(1)} %compare_and_fusion, bf16[64,8,8,128]{3,2,1,0:T(8,128)(2,1)S(1)} %fusion.14, bf16[512,128]{1,0:T(8,128)(2,1)S(1)} %get-tuple-element.10, bf16[512,128]{1,0:T(8,128)(2,1)S(1)} %collective-permute-done), kind=kOutput, calls=%fused_computation.4 | convolution fusion | flops 1086844928 | bytes 18628608 | tf_op jit(solution)/shard_map/thgd,shd->hgts/dot_general | solution.py:21
  268.2 4.0 %fusion.3 = f32[8,512]{1,0:T(8,128)S(1)} fusion(f32[1024,512,8]{1,0,2:T(8,128)S(1)} %get-tuple-element.14, f32[8,512]{1,0:T(8,128)S(1)} %get-tuple-element.13, pred[512,1024]{0,1:T(8,128)(4,1)S(1)} %compare_and_fusion), kind=kLoop, calls=%fused_computation.5 | loop fusion | flops 20967424 | bytes 17334272 | tf_op jit(solution)/shard_map/reduce_sum | solution.py:27
  272.2 0.0 collective-permute-done.1
  272.2 4.3 %divide_convert_fusion = bf16[8,512,128]{1,2,0:T(8,128)(2,1)S(1)} fusion(f32[8,512]{1,0:T(8,128)S(1)} %fusion.3, f32[1024,512,8]{1,0,2:T(8,128)S(1)} %get-tuple-element.14, f32[8,512]{1,0:T(8,128)S(1)} %get-tuple-element.13, pred[512,1024]{0,1:T(8,128)(4,1)S(1)} %compare_and_fusion, bf16[512,128]{1,0:T(8,128)(2,1)S(1)} %get-tuple-element.9, ...), kind=kOutput, calls=%fused_computation.13 | convolution fusion | flops 1096286208 | bytes 18644992 | tf_op jit(solution)/shard_map/hgts,shd->hgtd/dot_general | solution.py:29
  276.6 1.3 copy.9
  (4 shorter events, 0.0 us)
Async XLA Ops:
  241.5 30.7 %collective-permute-start.1 = (bf16[512,128]{1,0:T(8,128)(2,1)S(1)}, bf16[512,128]{1,0:T(8,128)(2,1)S(1)}, u32[]{:S(2)}, u32[]{:S(2)}) collective-permute-start(bf16[512,128]{1,0:T(8,128)(2,1)S(1)} %get-tuple-element.9), channel_id=1, source_target_pairs={{0,4},{4,8},{8,12},{12,16},{16,20},{20,24},{24,28},{1,5},{5,9},{9,... | collective-permute-start | bytes 393224 | tf_op jit(solution)/shard_map/ppermute | solution.py:16
  244.0 21.3 %collective-permute-start = (bf16[512,128]{1,0:T(8,128)(2,1)S(1)}, bf16[512,128]{1,0:T(8,128)(2,1)S(1)}, u32[]{:S(2)}, u32[]{:S(2)}) collective-permute-start(bf16[512,128]{1,0:T(8,128)(2,1)S(1)} %get-tuple-element.10), channel_id=1, source_target_pairs={{0,4},{4,8},{8,12},{12,16},{16,20},{20,24},{24,28},{1,5},{5,9},{9,... | collective-permute-start | bytes 393224 | tf_op jit(solution)/shard_map/ppermute | solution.py:16

commit v2 on v0

--- a/solution.py
+++ b/solution.py
@@ -1,6 +1,10 @@
+import functools
+
 import jax
 import jax.numpy as jnp
 from jax import lax
+from jax.experimental import pallas as pl
+from jax.experimental.pallas import tpu as pltpu
 from jax.sharding import PartitionSpec as P
 
 HEAD_DIMENSION = 128
@@ -28,19 +32,180 @@
     return jnp.transpose(result, (2, 0, 1, 3)).reshape(rows, -1).astype(jnp.bfloat16)
 
 
+MESH = pl.DeviceIdType.MESH
+
+
+def gather_kernel(lines, pieces, tok, wgt, mine, theirs, wgt_all, loc, ts, tr,
+                  up_s, up_r, dn_s, dn_r, y_s, y_r):
+    ctx, kv = lax.axis_index("ctx"), lax.axis_index("kv")
+    z, y = ctx // 2, ctx % 2
+    up, down, across = {"ctx": ctx + 2}, {"ctx": ctx - 2}, {"ctx": z * 2 + (1 - y)}
+    other_core, other_chip = (kv // 2) * 2 + (1 - kv % 2), (1 - kv // 2) * 2 + kv % 2
+    core, far = {"kv": other_core}, {"kv": other_chip}
+    has_up, has_down = z < lines - 1, z > 0
+    height, depth = tok.shape[1], wgt.shape[1]
+    rows = depth // pieces
+
+    barrier = pltpu.get_barrier_semaphore()
+    for other in (across, core, far):
+        pl.semaphore_signal(barrier, inc=1, device_id=other, device_id_type=MESH)
+
+    @pl.when(has_up)
+    def _():
+        pl.semaphore_signal(barrier, inc=1, device_id=up, device_id_type=MESH)
+
+    @pl.when(has_down)
+    def _():
+        pl.semaphore_signal(barrier, inc=1, device_id=down, device_id_type=MESH)
+
+    pl.semaphore_wait(barrier, 3 + has_up.astype(jnp.int32) + has_down.astype(jnp.int32))
+
+    def copy(src, dst, send, recv, other):
+        return pltpu.make_async_remote_copy(
+            src_ref=src, dst_ref=dst, send_sem=send, recv_sem=recv,
+            device_id=other, device_id_type=MESH)
+
+    def place(line, side, p):
+        start = pl.multiple_of((line * 2 + side) * depth + p * rows, rows)
+        return wgt_all.at[pl.ds(start, rows), :]
+
+    def own(half, p):
+        return wgt.at[half, pl.ds(p * rows, rows), :]
+
+    def block(off, s, p):
+        return own(y, p) if (off, s) == (0, 0) else place(z + off, y if s == 0 else 1 - y, p)
+
+    def up_copy(d, s, p):
+        dst = place(z - d, y if s == 0 else 1 - y, p)
+        return copy(block(-d, s, p), dst, up_s.at[d, s, p], up_r.at[d, s, p], up)
+
+    def down_copy(d, s, p):
+        dst = place(z + d, y if s == 0 else 1 - y, p)
+        return copy(block(d, s, p), dst, dn_s.at[d, s, p], dn_r.at[d, s, p], down)
+
+    def y_copy(p):
+        return copy(own(1 - y, p), place(z, y, p), y_s.at[p], y_r.at[p], across)
+
+    def columns(ref, k):
+        return ref.at[:, pl.ds(pl.multiple_of(k * height, height), height)]
+
+    def both_ways(d, s, p):
+        pl.when(has_up)(lambda: up_copy(d, s, p).start())
+        pl.when(has_down)(lambda: down_copy(d, s, p).start())
+
+    own_far = copy(tok, columns(mine, kv), ts.at[0], tr.at[0], far)
+    own_core = copy(tok, columns(mine, kv), ts.at[1], tr.at[1], core)
+    own_across = copy(tok, columns(theirs, kv), ts.at[2], tr.at[2], across)
+    mine_core = copy(columns(mine, other_chip), columns(mine, other_chip), ts.at[3], tr.at[3], core)
+    their_far = copy(columns(theirs, kv), columns(theirs, kv), ts.at[4], tr.at[4], far)
+    their_core = copy(columns(theirs, kv), columns(theirs, kv), ts.at[5], tr.at[5], core)
+    last_core = copy(columns(theirs, other_chip), columns(theirs, other_chip), ts.at[6], tr.at[6], core)
+
+    for p in range(pieces):
+        y_copy(p).start()
+        both_ways(0, 0, p)
+    own_far.start()
+    own_across.start()
+    own_core.start()
+    local = [pltpu.make_async_copy(tok, columns(mine, kv), loc.at[0]),
+             pltpu.make_async_copy(
+                 wgt.at[y], wgt_all.at[pl.ds(pl.multiple_of(ctx * depth, depth), depth), :], loc.at[1])]
+    for c in local:
+        c.start()
+    for p in range(pieces):
+        y_copy(p).wait_recv()
+        both_ways(0, 1, p)
+
+    def relay_mine():
+        own_far.wait_recv()
+        mine_core.start()
+
+    def relay_theirs():
+        own_across.wait_recv()
+        their_far.start()
+        their_core.start()
+
+    def relay_last():
+        their_far.wait_recv()
+        last_core.start()
+
+    relays = {(1, 1): relay_mine, (2, 0): relay_theirs, (3, 0): relay_last}
+    for d in range(1, lines):
+        for s in range(2):
+            for p in range(pieces):
+                @pl.when(z >= d)
+                def _(d=d, s=s, p=p):
+                    up_copy(d - 1, s, p).wait_recv()
+                    if d < lines - 1:
+                        pl.when(has_up)(lambda: up_copy(d, s, p).start())
+
+                @pl.when(z + d < lines)
+                def _(d=d, s=s, p=p):
+                    down_copy(d - 1, s, p).wait_recv()
+                    if d < lines - 1:
+                        pl.when(has_down)(lambda: down_copy(d, s, p).start())
+            if (d, s) in relays:
+                relays.pop((d, s))()
+    for key in sorted(relays):
+        relays[key]()
+
+    for c in (own_core, mine_core, their_core, last_core):
+        c.wait_recv()
+    for c in (own_far, own_core, own_across, mine_core, their_far, their_core, last_core):
+        c.wait_send()
+    for c in local:
+        c.wait()
+    for p in range(pieces):
+        y_copy(p).wait_send()
+        for s in range(2):
+            for d in range(lines - 1):
+                pl.when(has_up & (z >= d))(lambda d=d, s=s, p=p: up_copy(d, s, p).wait_send())
+                pl.when(has_down & (z + d < lines))(
+                    lambda d=d, s=s, p=p: down_copy(d, s, p).wait_send())
+
+
+def gathered(tokens, weights):
+    lines = lax.axis_size("ctx") // 2
+    _, depth, width = weights.shape
+    pieces = max(1, depth // 256)
+    dma = pltpu.SemaphoreType.DMA
+    line_sems = [dma((lines, 2, pieces))] * 4
+    all_features = jax.ShapeDtypeStruct(
+        (tokens.shape[0], tokens.shape[1] * lax.axis_size("kv")), tokens.dtype)
+    return pl.pallas_call(
+        functools.partial(gather_kernel, lines, pieces),
+        out_shape=(
+            all_features,
+            all_features,
+            jax.ShapeDtypeStruct((depth * lax.axis_size("ctx"), width), weights.dtype),
+        ),
+        in_specs=[pl.BlockSpec(memory_space=pl.ANY)] * 2,
+        out_specs=[pl.BlockSpec(memory_space=pl.ANY)] * 3,
+        scratch_shapes=[dma((2,)), dma((7,)), dma((7,))] + line_sems + [dma((pieces,))] * 2,
+        compiler_params=pltpu.CompilerParams(collective_id=0, has_side_effects=True),
+    )(tokens, weights)
+
+
 def shards(tokens, segment_ids, query_weight, key_weight, value_projection_matrix):
-    whole = lax.all_gather(tokens, "kv", axis=1, tiled=True)
-    rows = whole.shape[0]
-
-    def add_rows(piece):
-        return jnp.dot(whole, piece, preferred_element_type=jnp.float32)
-
-    q_sum = add_rows(lax.all_gather(query_weight, "ctx", axis=0, tiled=True))
-    k_sum = add_rows(lax.all_gather(key_weight, "ctx", axis=0, tiled=True))
-    v_sum = add_rows(lax.all_gather(value_projection_matrix, "ctx", axis=0, tiled=True))
-    query_rows = q_sum.astype(jnp.bfloat16)
-    key_rows = k_sum.astype(jnp.bfloat16)
-    value_rows = v_sum.astype(jnp.bfloat16)
+    rows = tokens.shape[0]
+    wide, half = key_weight.shape[1], query_weight.shape[1] // 2
+    packed = jnp.stack([
+        jnp.concatenate([key_weight, query_weight[:, :half]], axis=1),
+        jnp.concatenate([value_projection_matrix, query_weight[:, half:]], axis=1),
+    ])
+    mine, theirs, weights = gathered(tokens, packed)
+
+    def project(whole):
+        return jnp.dot(whole, weights, preferred_element_type=jnp.float32).astype(jnp.bfloat16)
+
+    pairs = [(i, i ^ 1) for i in range(lax.axis_size("ctx"))]
+    received = lax.ppermute(project(theirs), "ctx", pairs)
+    kept = project(mine)
+    first_side = lax.axis_index("ctx") % 2 == 0
+    low = jnp.where(first_side, kept, received)
+    high = jnp.where(first_side, received, kept)
+    key_rows, value_rows = low[:, :wide], high[:, :wide]
+    query_rows = jnp.concatenate([low[:, wide:], high[:, wide:]], axis=1)
     prev_key, prev_value = shifted((key_rows, value_rows), "ctx", 1)
     kv_heads = key_weight.shape[1] // HEAD_DIMENSION
     query_group = query_weight.shape[1] // (HEAD_DIMENSION * kv_heads)

time: 435 us -> 240 us (0.55)
  waiting for transfers between devices: 373 us -> 13.8 us
  Pallas kernels: 0 us -> 175 us
  between operations: 13.2 us -> 0.12 us
    all_gather x4 -> x0, waiting for transfers between devices: 371 us -> none  [the longest x1 219 us: shards(): q_sum = add_rows(lax.all_gather(query_weight, 'ctx', axis=0, tiled=True))]
    pallas_call x0 -> x1, Pallas kernels: none -> 175 us  [gathered(): pl.pallas_call(functools.partial(gather_kernel, lines, pieces), out_shape...]
    ppermute x0 -> x1, waiting for transfers between devices: none -> 13.2 us  [shards(): received = lax.ppermute(project(theirs), 'ctx', pairs)]
    dot_general x3 -> x2, matrix products: 27.4 us -> 24.3 us  [project(): jnp.dot(whole, weights, preferred_element_type=jnp.float32)]
  transfers between devices with their start and end apart: 6 -> 3, of which waited for: 4 -> 2; matrix products, arithmetic and copies ran while one was open for 8% -> 4% of each run, Pallas kernels for 0% -> 0%
where the time goes in v2:
time: 240 us
  Pallas kernels  175 us (73%)
  matrix products  31.5 us (13%)
  waiting for transfers between devices  13.8 us (6%)
  other arithmetic  8.13 us (3%)
  starting transfers between devices  7.12 us (3%)
  local copies, waits for them, and re-layouts  3.93 us (2%)
    pallas_call x1, Pallas kernels, gathered(): pl.pallas_call(functools.partial(gather_kernel, lines, pieces), out_shape...  175 us
    dot_general x2, matrix products, project(): jnp.dot(whole, weights, preferred_element_type=jnp.float32)  24.3 us
    ppermute x1, waiting for transfers between devices, shards(): received = lax.ppermute(project(theirs), 'ctx', pairs)  13.2 us
    ppermute x2, starting transfers between devices, shifted(): return lax.ppermute(shard, axis, pairs)  5.53 us
  transfers between devices with their start and end apart: 3, of which 2 were waited for; matrix products, arithmetic and copies ran while one was open for 4% of the time, Pallas kernels for 0%

profile of v2, /device:TPU:0, one launch (start us, length us, event | category | flops | bytes accessed | tf_op | source)
XLA Modules:
  0.0 239.9 jit_solution(16235851423936630328)
XLA Ops:
  0.0 1.7 fusion.21
  1.7 1.3 maximum_bitcast_fusion
  3.0 1.8 pad_maximum_fusion.wgt
  4.8 175.3 %shard_map.55 = (bf16[512,8192]{1,0:T(8,128)(2,1)}, bf16[512,8192]{1,0:T(8,128)(2,1)}, bf16[8192,640]{1,0:T(8,128)(2,1)}) custom-call(bf16[512,2048]{1,0:T(8,128)(2,1)} %tok.1, bf16[2,1024,640]{2,1,0:T(8,128)(2,1)} %pad_maximum_fusion.wgt), custom_call_target="tpu_custom_call" | custom-call | tf_op jit(solution)/shard_map/pallas_call | solution.py:175
  180.1 12.1 %convolution_convert_fusion = bf16[512,640]{1,0:T(8,128)(2,1)S(1)} fusion(bf16[512,8192]{1,0:T(8,128)(2,1)} %get-tuple-element.10, bf16[8192,640]{1,0:T(8,128)(2,1)} %get-tuple-element.9), kind=kOutput, calls=%fused_computation.11 | convolution fusion | flops 5369036800 | bytes 19529728 | tf_op jit(solution)/shard_map/dot_general | solution.py:199
  192.3 1.6 collective-permute-start
  193.9 0.8 fusion.22
  194.7 13.2 %collective-permute-done = bf16[512,640]{1,0:T(8,128)(2,1)S(1)} collective-permute-done((bf16[512,640]{1,0:T(8,128)(2,1)S(1)}, bf16[512,640]{1,0:T(8,128)(2,1)S(1)}, u32[]{:S(2)}, u32[]{:S(2)}) %collective-permute-start) | collective-permute-done | bytes 655392 | tf_op jit(solution)/shard_map/ppermute | solution.py:202
  207.9 12.1 %broadcast_select_fusion.1 = (bf16[512,640]{1,0:T(8,128)(2,1)S(1)}, bf16[512,640]{1,0:T(8,128)(2,1)S(1)}) fusion(bf16[512,640]{1,0:T(8,128)(2,1)S(1)} %collective-permute-done, pred[]{:T(512)S(6)} %eq.25, bf16[512,8192]{1,0:T(8,128)(2,1)} %get-tuple-element.8, bf16[8192,640]{1,0:T(8,128)(2,1)} %get-tuple-element.9), kind=kOutput, calls=%fused_computation.20 | convolution fusion | flops 5369692160 | bytes 20840448 | tf_op jit(solution)/shard_map/dot_general | solution.py:199
  220.1 3.4 %collective-permute-start.1 = (bf16[512,128]{1,0:T(8,128)(2,1)S(1)}, bf16[512,128]{1,0:T(8,128)(2,1)S(1)}, u32[]{:S(2)}, u32[]{:S(2)}) collective-permute-start(bf16[512,128]{1,0:T(8,128)(2,1)S(1)} %slice.24), channel_id=1, source_target_pairs={{0,4},{4,8},{8,12},{12,16},{16,20},{20,24},{24,28},{1,5},{5,9},{9,... | collective-permute-start | bytes 393224 | tf_op jit(solution)/shard_map/ppermute | solution.py:16
  223.5 1.0 compare_and_fusion
  224.6 2.1 collective-permute-start.2
  226.7 0.6 collective-permute-done.1
  227.3 2.9 %fusion = (f32[8,512]{1,0:T(8,128)S(1)}, f32[1024,512,8]{1,0,2:T(8,128)S(1)}) fusion(pred[512,1024]{0,1:T(8,128)(4,1)S(1)} %compare_and_fusion, bf16[512,128]{1,0:T(8,128)(2,1)S(1)} %slice.24, bf16[512,128]{1,0:T(8,128)(2,1)S(1)} %collective-permute-done.1, bf16[512,512]{1,0:T(8,128)(2,1)S(1)} %slice.26, bf16[512,512]{1,0:T(8,128)(2,1)S(1)} %slice.25), kind=kOutput, calls=%fused_computation.2 | convolution fusion | flops 1088942080 | bytes 18628608 | tf_op jit(solution)/shard_map/thgd,shd->hgts/dot_general | solution.py:21
  230.2 4.0 %fusion.1 = f32[8,512]{1,0:T(8,128)S(1)} fusion(f32[1024,512,8]{1,0,2:T(8,128)S(1)} %get-tuple-element.18, f32[8,512]{1,0:T(8,128)S(1)} %get-tuple-element.17, pred[512,1024]{0,1:T(8,128)(4,1)S(1)} %compare_and_fusion), kind=kLoop, calls=%fused_computation.3 | loop fusion | flops 20967424 | bytes 17334272 | tf_op jit(solution)/shard_map/reduce_sum | solution.py:27
  234.2 0.0 collective-permute-done.2
  234.2 4.3 %divide_convert_fusion = bf16[8,512,128]{1,2,0:T(8,128)(2,1)S(1)} fusion(f32[8,512]{1,0:T(8,128)S(1)} %fusion.1, f32[1024,512,8]{1,0,2:T(8,128)S(1)} %get-tuple-element.18, f32[8,512]{1,0:T(8,128)S(1)} %get-tuple-element.17, pred[512,1024]{0,1:T(8,128)(4,1)S(1)} %compare_and_fusion, bf16[512,128]{1,0:T(8,128)(2,1)S(1)} %slice.27, ...), kind=kOutput, calls=%fused_computation.9 | convolution fusion | flops 1096286208 | bytes 18644992 | tf_op jit(solution)/shard_map/hgts,shd->hgtd/dot_general | solution.py:29
  238.6 1.3 copy.9
  (7 shorter events, 0.1 us)
Async XLA Ops:
  192.3 15.7 %collective-permute-start = (bf16[512,640]{1,0:T(8,128)(2,1)S(1)}, bf16[512,640]{1,0:T(8,128)(2,1)S(1)}, u32[]{:S(2)}, u32[]{:S(2)}) collective-permute-start(bf16[512,640]{1,0:T(8,128)(2,1)S(1)} %convolution_convert_fusion), channel_id=1, source_target_pairs={{0,4},{4,0},{8,12},{12,8},{16,20},{20,16},{24,28},{28,24},{1,5},{5... | collective-permute-start | bytes 1966088 | tf_op jit(solution)/shard_map/ppermute | solution.py:202
  220.1 7.2 %collective-permute-start.1 = (bf16[512,128]{1,0:T(8,128)(2,1)S(1)}, bf16[512,128]{1,0:T(8,128)(2,1)S(1)}, u32[]{:S(2)}, u32[]{:S(2)}) collective-permute-start(bf16[512,128]{1,0:T(8,128)(2,1)S(1)} %slice.24), channel_id=1, source_target_pairs={{0,4},{4,8},{8,12},{12,16},{16,20},{20,24},{24,28},{1,5},{5,9},{9,... | collective-permute-start | bytes 393224 | tf_op jit(solution)/shard_map/ppermute | solution.py:16
  224.6 9.6 %collective-permute-start.2 = (bf16[512,128]{1,0:T(8,128)(2,1)S(1)}, bf16[512,128]{1,0:T(8,128)(2,1)S(1)}, u32[]{:S(2)}, u32[]{:S(2)}) collective-permute-start(bf16[512,128]{1,0:T(8,128)(2,1)S(1)} %slice.27), channel_id=1, source_target_pairs={{0,4},{4,8},{8,12},{12,16},{16,20},{20,24},{24,28},{1,5},{5,9},{9,... | collective-permute-start | bytes 393224 | tf_op jit(solution)/shard_map/ppermute | solution.py:16

commit v3 on v2

--- a/solution.py
+++ b/solution.py
@@ -200,7 +200,7 @@
 
     pairs = [(i, i ^ 1) for i in range(lax.axis_size("ctx"))]
     received = lax.ppermute(project(theirs), "ctx", pairs)
-    kept = project(mine)
+    kept, received = lax.optimization_barrier((project(mine), received))
     first_side = lax.axis_index("ctx") % 2 == 0
     low = jnp.where(first_side, kept, received)
     high = jnp.where(first_side, received, kept)

time: 240 us -> 228 us (0.950)
  waiting for transfers between devices: 13.8 us -> 7.11 us
  matrix products: 31.5 us -> 26.1 us
    ppermute x1, waiting for transfers between devices: 13.2 us -> 6.52 us  [shards(): received = lax.ppermute(project(theirs), 'ctx', pairs)]
    dot_general x2, matrix products: 24.3 us -> 18.9 us  [project(): jnp.dot(whole, weights, preferred_element_type=jnp.float32)]
  transfers between devices with their start and end apart: 3 -> 3, of which waited for: 2 -> 2; matrix products, arithmetic and copies ran while one was open for 4% -> 7% of each run, Pallas kernels for 0% -> 0%
where the time goes in v3:
time: 228 us
  Pallas kernels  175 us (77%)
  matrix products  26.1 us (11%)
  other arithmetic  8.27 us (4%)
  starting transfers between devices  7.12 us (3%)
  waiting for transfers between devices  7.11 us (3%)
  local copies, waits for them, and re-layouts  3.94 us (2%)
    pallas_call x1, Pallas kernels, gathered(): pl.pallas_call(functools.partial(gather_kernel, lines, pieces), out_shape...  175 us
    dot_general x2, matrix products, project(): jnp.dot(whole, weights, preferred_element_type=jnp.float32)  18.9 us
    ppermute x1, waiting for transfers between devices, shards(): received = lax.ppermute(project(theirs), 'ctx', pairs)  6.52 us
    ppermute x2, starting transfers between devices, shifted(): return lax.ppermute(shard, axis, pairs)  5.53 us
  transfers between devices with their start and end apart: 3, of which 2 were waited for; matrix products, arithmetic and copies ran while one was open for 7% of the time, Pallas kernels for 0%

profile of v3, /device:TPU:0, one launch (start us, length us, event | category | flops | bytes accessed | tf_op | source)
XLA Modules:
  0.0 228.0 jit_solution(9903191649513470068)
XLA Ops:
  0.0 1.7 fusion.21
  1.7 1.3 maximum_bitcast_fusion
  3.0 1.8 pad_maximum_fusion.wgt
  4.8 175.3 %shard_map.55 = (bf16[512,8192]{1,0:T(8,128)(2,1)}, bf16[512,8192]{1,0:T(8,128)(2,1)}, bf16[8192,640]{1,0:T(8,128)(2,1)}) custom-call(bf16[512,2048]{1,0:T(8,128)(2,1)} %tok.1, bf16[2,1024,640]{2,1,0:T(8,128)(2,1)} %pad_maximum_fusion.wgt), custom_call_target="tpu_custom_call" | custom-call | tf_op jit(solution)/shard_map/pallas_call | solution.py:175
  180.1 0.0 copy-start
  180.1 0.0 copy-start.1
  180.2 12.3 %convolution_convert_fusion = bf16[512,640]{1,0:T(8,128)(2,1)S(1)} fusion(bf16[512,8192]{1,0:T(8,128)(2,1)} %get-tuple-element.12, bf16[8192,640]{1,0:T(8,128)(2,1)} %get-tuple-element.11), kind=kOutput, calls=%fused_computation.11 | convolution fusion | flops 5369036800 | bytes 19529728 | tf_op jit(solution)/shard_map/dot_general | solution.py:199
  192.4 1.6 collective-permute-start
  194.0 0.0 copy-done
  194.0 0.0 copy-done.1
  194.0 6.7 %convolution_convert_fusion.1 = bf16[512,640]{1,0:T(8,128)(2,1)S(1)} fusion(bf16[512,8192]{1,0:T(8,128)(2,1)S(1)} %copy-done.1, bf16[8192,640]{1,0:T(8,128)(2,1)S(1)} %copy-done), kind=kOutput, calls=%fused_computation.12 | convolution fusion | flops 5369036800 | bytes 19529728 | tf_op jit(solution)/shard_map/dot_general | solution.py:199
  200.7 0.8 fusion.22
  201.6 6.5 %collective-permute-done = bf16[512,640]{1,0:T(8,128)(2,1)S(1)} collective-permute-done((bf16[512,640]{1,0:T(8,128)(2,1)S(1)}, bf16[512,640]{1,0:T(8,128)(2,1)S(1)}, u32[]{:S(2)}, u32[]{:S(2)}) %collective-permute-start) | collective-permute-done | bytes 655392 | tf_op jit(solution)/shard_map/ppermute | solution.py:202
  208.1 0.1 broadcast_select_fusion.1
  208.2 3.4 %collective-permute-start.1 = (bf16[512,128]{1,0:T(8,128)(2,1)S(1)}, bf16[512,128]{1,0:T(8,128)(2,1)S(1)}, u32[]{:S(2)}, u32[]{:S(2)}) collective-permute-start(bf16[512,128]{1,0:T(8,128)(2,1)S(1)} %slice.24), channel_id=1, source_target_pairs={{0,4},{4,8},{8,12},{12,16},{16,20},{20,24},{24,28},{1,5},{5,9},{9,... | collective-permute-start | bytes 393224 | tf_op jit(solution)/shard_map/ppermute | solution.py:16
  211.7 1.0 compare_and_fusion
  212.8 2.1 collective-permute-start.2
  214.9 0.6 collective-permute-done.1
  215.5 2.9 %fusion = (f32[8,512]{1,0:T(8,128)S(1)}, f32[1024,512,8]{1,0,2:T(8,128)S(1)}) fusion(pred[512,1024]{0,1:T(8,128)(4,1)S(1)} %compare_and_fusion, bf16[512,128]{1,0:T(8,128)(2,1)S(1)} %slice.24, bf16[512,128]{1,0:T(8,128)(2,1)S(1)} %collective-permute-done.1, bf16[512,512]{1,0:T(8,128)(2,1)S(1)} %slice.26, bf16[512,512]{1,0:T(8,128)(2,1)S(1)} %slice.25), kind=kOutput, calls=%fused_computation.2 | convolution fusion | flops 1088942080 | bytes 18628608 | tf_op jit(solution)/shard_map/thgd,shd->hgts/dot_general | solution.py:21
  218.3 4.0 %fusion.1 = f32[8,512]{1,0:T(8,128)S(1)} fusion(f32[1024,512,8]{1,0,2:T(8,128)S(1)} %get-tuple-element.22, f32[8,512]{1,0:T(8,128)S(1)} %get-tuple-element.21, pred[512,1024]{0,1:T(8,128)(4,1)S(1)} %compare_and_fusion), kind=kLoop, calls=%fused_computation.3 | loop fusion | flops 20967424 | bytes 17334272 | tf_op jit(solution)/shard_map/reduce_sum | solution.py:27
  222.4 0.0 collective-permute-done.2
  222.4 4.3 %divide_convert_fusion = bf16[8,512,128]{1,2,0:T(8,128)(2,1)S(1)} fusion(f32[8,512]{1,0:T(8,128)S(1)} %fusion.1, f32[1024,512,8]{1,0,2:T(8,128)S(1)} %get-tuple-element.22, f32[8,512]{1,0:T(8,128)S(1)} %get-tuple-element.21, pred[512,1024]{0,1:T(8,128)(4,1)S(1)} %compare_and_fusion, bf16[512,128]{1,0:T(8,128)(2,1)S(1)} %slice.27, ...), kind=kOutput, calls=%fused_computation.9 | convolution fusion | flops 1096286208 | bytes 18644992 | tf_op jit(solution)/shard_map/hgts,shd->hgtd/dot_general | solution.py:29
  226.7 1.3 copy.9
  (7 shorter events, 0.1 us)
Async XLA Ops:
  180.1 13.9 %copy-start = (bf16[8192,640]{1,0:T(8,128)(2,1)S(1)}, bf16[8192,640]{1,0:T(8,128)(2,1)}, u32[]{:S(2)}) copy-start(bf16[8192,640]{1,0:T(8,128)(2,1)} %get-tuple-element.11) | copy-start | bytes 31457284
  180.1 13.9 %copy-start.1 = (bf16[512,8192]{1,0:T(8,128)(2,1)S(1)}, bf16[512,8192]{1,0:T(8,128)(2,1)}, u32[]{:S(2)}) copy-start(bf16[512,8192]{1,0:T(8,128)(2,1)} %get-tuple-element.10) | copy-start | bytes 25165828
  192.4 15.7 %collective-permute-start = (bf16[512,640]{1,0:T(8,128)(2,1)S(1)}, bf16[512,640]{1,0:T(8,128)(2,1)S(1)}, u32[]{:S(2)}, u32[]{:S(2)}) collective-permute-start(bf16[512,640]{1,0:T(8,128)(2,1)S(1)} %convolution_convert_fusion), channel_id=1, source_target_pairs={{0,4},{4,0},{8,12},{12,8},{16,20},{20,16},{24,28},{28,24},{1,5},{5... | collective-permute-start | bytes 1966088 | tf_op jit(solution)/shard_map/ppermute | solution.py:202
  208.2 7.2 %collective-permute-start.1 = (bf16[512,128]{1,0:T(8,128)(2,1)S(1)}, bf16[512,128]{1,0:T(8,128)(2,1)S(1)}, u32[]{:S(2)}, u32[]{:S(2)}) collective-permute-start(bf16[512,128]{1,0:T(8,128)(2,1)S(1)} %slice.24), channel_id=1, source_target_pairs={{0,4},{4,8},{8,12},{12,16},{16,20},{20,24},{24,28},{1,5},{5,9},{9,... | collective-permute-start | bytes 393224 | tf_op jit(solution)/shard_map/ppermute | solution.py:16
  212.8 9.6 %collective-permute-start.2 = (bf16[512,128]{1,0:T(8,128)(2,1)S(1)}, bf16[512,128]{1,0:T(8,128)(2,1)S(1)}, u32[]{:S(2)}, u32[]{:S(2)}) collective-permute-start(bf16[512,128]{1,0:T(8,128)(2,1)S(1)} %slice.27), channel_id=1, source_target_pairs={{0,4},{4,8},{8,12},{12,16},{16,20},{20,24},{24,28},{1,5},{5,9},{9,... | collective-permute-start | bytes 393224 | tf_op jit(solution)/shard_map/ppermute | solution.py:16

commit v4 on v3

--- a/solution.py
+++ b/solution.py
@@ -35,7 +35,7 @@
 MESH = pl.DeviceIdType.MESH
 
 
-def gather_kernel(lines, pieces, tok, wgt, mine, theirs, wgt_all, loc, ts, tr,
+def gather_kernel(lines, pieces, tok, wgt, zeros, mine, theirs, wgt_all, ext_mine, ext_theirs, loc, ts, tr,
                   up_s, up_r, dn_s, dn_r, y_s, y_r):
     ctx, kv = lax.axis_index("ctx"), lax.axis_index("kv")
     z, y = ctx // 2, ctx % 2
@@ -107,6 +107,20 @@
     own_far.start()
     own_across.start()
     own_core.start()
+    edge, inner = (z == 0) | (z == lines - 1), (z == 1) | (z == lines - 2)
+    core_index, strip = kv % 2, tok.shape[0] // 2
+    opposite = (lines - 1) * (1 - jnp.minimum(z, 1))
+    strip_rows = pl.ds(pl.multiple_of(core_index * strip, strip), strip)
+    needed = pl.ds(pl.multiple_of(opposite * 2 * depth, 2 * depth), 2 * depth)
+
+    def edge_copy(other):
+        return copy(mine.at[strip_rows, needed], ext_mine.at[strip_rows, :], ts.at[7], tr.at[7], other)
+
+    ext_across = copy(ext_mine.at[strip_rows, :], ext_theirs.at[strip_rows, :], ts.at[8], tr.at[8], across)
+    ext_core = copy(ext_mine.at[strip_rows, :], ext_mine.at[strip_rows, :], ts.at[9], tr.at[9], core)
+    ext_last = copy(ext_theirs.at[strip_rows, :], ext_theirs.at[strip_rows, :], ts.at[10], tr.at[10], core)
+    fill = pltpu.make_async_copy(zeros, wgt_all.at[needed, :], loc.at[2])
+    pl.when(edge)(lambda: fill.start())
     local = [pltpu.make_async_copy(tok, columns(mine, kv), loc.at[0]),
              pltpu.make_async_copy(
                  wgt.at[y], wgt_all.at[pl.ds(pl.multiple_of(ctx * depth, depth), depth), :], loc.at[1])]
@@ -119,46 +133,70 @@
     def relay_mine():
         own_far.wait_recv()
         mine_core.start()
+        own_core.wait_recv()
+        mine_core.wait_recv()
+        local[0].wait()
+        pl.when(z == 0)(lambda: edge_copy(up).start())
+        pl.when(z == lines - 1)(lambda: edge_copy(down).start())
 
     def relay_theirs():
         own_across.wait_recv()
         their_far.start()
         their_core.start()
 
-    def relay_last():
-        their_far.wait_recv()
-        last_core.start()
-
-    relays = {(1, 1): relay_mine, (2, 0): relay_theirs, (3, 0): relay_last}
-    for d in range(1, lines):
+    def relay_ext():
+        @pl.when(inner)
+        def _():
+            edge_copy(core).wait_recv()
+            ext_across.start()
+            ext_core.start()
+
+    relays = {(1, 0): relay_mine, (1, 1): relay_theirs, (2, 0): relay_ext}
+    for d in range(1, lines - 1):
         for s in range(2):
             for p in range(pieces):
                 @pl.when(z >= d)
                 def _(d=d, s=s, p=p):
                     up_copy(d - 1, s, p).wait_recv()
-                    if d < lines - 1:
+                    if d < lines - 2:
                         pl.when(has_up)(lambda: up_copy(d, s, p).start())
 
                 @pl.when(z + d < lines)
                 def _(d=d, s=s, p=p):
                     down_copy(d - 1, s, p).wait_recv()
-                    if d < lines - 1:
+                    if d < lines - 2:
                         pl.when(has_down)(lambda: down_copy(d, s, p).start())
             if (d, s) in relays:
                 relays.pop((d, s))()
     for key in sorted(relays):
         relays[key]()
 
-    for c in (own_core, mine_core, their_core, last_core):
+    their_far.wait_recv()
+    last_core.start()
+
+    @pl.when(inner)
+    def _():
+        ext_across.wait_recv()
+        ext_last.start()
+        ext_core.wait_recv()
+        ext_last.wait_recv()
+        for c in (ext_across, ext_core, ext_last):
+            c.wait_send()
+
+    @pl.when(edge)
+    def _():
+        edge_copy(core).wait_send()
+        fill.wait()
+
+    for c in (their_core, last_core):
         c.wait_recv()
     for c in (own_far, own_core, own_across, mine_core, their_far, their_core, last_core):
         c.wait_send()
-    for c in local:
-        c.wait()
+    local[1].wait()
     for p in range(pieces):
         y_copy(p).wait_send()
         for s in range(2):
-            for d in range(lines - 1):
+            for d in range(lines - 2):
                 pl.when(has_up & (z >= d))(lambda d=d, s=s, p=p: up_copy(d, s, p).wait_send())
                 pl.when(has_down & (z + d < lines))(
                     lambda d=d, s=s, p=p: down_copy(d, s, p).wait_send())
@@ -172,18 +210,21 @@
     line_sems = [dma((lines, 2, pieces))] * 4
     all_features = jax.ShapeDtypeStruct(
         (tokens.shape[0], tokens.shape[1] * lax.axis_size("kv")), tokens.dtype)
+    strip = jax.ShapeDtypeStruct((tokens.shape[0], 2 * depth), tokens.dtype)
     return pl.pallas_call(
         functools.partial(gather_kernel, lines, pieces),
         out_shape=(
             all_features,
             all_features,
             jax.ShapeDtypeStruct((depth * lax.axis_size("ctx"), width), weights.dtype),
+            strip,
+            strip,
         ),
-        in_specs=[pl.BlockSpec(memory_space=pl.ANY)] * 2,
-        out_specs=[pl.BlockSpec(memory_space=pl.ANY)] * 3,
-        scratch_shapes=[dma((2,)), dma((7,)), dma((7,))] + line_sems + [dma((pieces,))] * 2,
+        in_specs=[pl.BlockSpec(memory_space=pl.ANY)] * 3,
+        out_specs=[pl.BlockSpec(memory_space=pl.ANY)] * 5,
+        scratch_shapes=[dma((3,)), dma((11,)), dma((11,))] + line_sems + [dma((pieces,))] * 2,
         compiler_params=pltpu.CompilerParams(collective_id=0, has_side_effects=True),
-    )(tokens, weights)
+    )(tokens, weights, jnp.zeros((2 * depth, width), weights.dtype))
 
 
 def shards(tokens, segment_ids, query_weight, key_weight, value_projection_matrix):
@@ -193,14 +234,26 @@
         jnp.concatenate([key_weight, query_weight[:, :half]], axis=1),
         jnp.concatenate([value_projection_matrix, query_weight[:, half:]], axis=1),
     ])
-    mine, theirs, weights = gathered(tokens, packed)
-
-    def project(whole):
-        return jnp.dot(whole, weights, preferred_element_type=jnp.float32).astype(jnp.bfloat16)
-
-    pairs = [(i, i ^ 1) for i in range(lax.axis_size("ctx"))]
-    received = lax.ppermute(project(theirs), "ctx", pairs)
-    kept, received = lax.optimization_barrier((project(mine), received))
+    mine, theirs, weights, ext_mine, ext_theirs = gathered(tokens, packed)
+    length, block = lax.axis_size("ctx"), 2 * query_weight.shape[0]
+    pairs = [(i, i ^ 1) for i in range(length)]
+    inward = [(2, 0), (3, 1), (length - 4, length - 2), (length - 3, length - 1)]
+    begin = jnp.where(lax.axis_index("ctx") // 2 == 1, weights.shape[0] - block, 0)
+    opposite = lax.dynamic_slice_in_dim(weights, begin, block, 0)
+
+    def project(whole, matrix):
+        return jnp.dot(whole, matrix, preferred_element_type=jnp.float32)
+
+    def help_end(ext):
+        return lax.ppermute(project(ext, opposite).astype(jnp.bfloat16), "ctx", inward)
+
+    def whole_sum(whole, helped):
+        own, helped = lax.optimization_barrier((project(whole, weights), helped))
+        return (own + helped.astype(jnp.float32)).astype(jnp.bfloat16)
+
+    helped_theirs, helped_mine = help_end(ext_theirs), help_end(ext_mine)
+    received = lax.ppermute(whole_sum(theirs, helped_theirs), "ctx", pairs)
+    kept = whole_sum(mine, helped_mine)
     first_side = lax.axis_index("ctx") % 2 == 0
     low = jnp.where(first_side, kept, received)
     high = jnp.where(first_side, received, kept)

time: 228 us -> 280 us (1.23)
  Pallas kernels: 175 us -> 200 us
  waiting for transfers between devices: 7.11 us -> 23.8 us
  matrix products: 26.1 us -> 32.8 us
    pallas_call x1, Pallas kernels: 175 us -> 200 us  [gathered(): pl.pallas_call(functools.partial(gather_kernel, lines, pieces), out_shape...]
    ppermute x1 -> x3, waiting for transfers between devices: 6.52 us -> 23.7 us  [the longest x2 16.7 us: help_end(): lax.ppermute(project(ext, opposite).astype(jnp.bfloat16), 'ctx', inward)]
    dot_general x2 -> x4, matrix products: 18.9 us -> 25.5 us  [project(): return jnp.dot(whole, matrix, preferred_element_type=jnp.float32)]
  transfers between devices with their start and end apart: 3 -> 5, of which waited for: 2 -> 2; matrix products, arithmetic and copies ran while one was open for 7% -> 10% of each run, Pallas kernels for 0% -> 0%
where the time goes in v4:
time: 280 us
  Pallas kernels  200 us (71%)
  matrix products  32.8 us (12%)
  waiting for transfers between devices  23.8 us (8%)
  starting transfers between devices  9.91 us (4%)
  other arithmetic  7.52 us (3%)
  local copies, waits for them, and re-layouts  5.67 us (2%)
    pallas_call x1, Pallas kernels, gathered(): pl.pallas_call(functools.partial(gather_kernel, lines, pieces), out_shape...  200 us
    dot_general x4, matrix products, project(): return jnp.dot(whole, matrix, preferred_element_type=jnp.float32)  25.5 us
    ppermute x2, waiting for transfers between devices, help_end(): lax.ppermute(project(ext, opposite).astype(jnp.bfloat16), 'ctx', inward)  16.7 us
    ppermute x1, waiting for transfers between devices, shards(): received = lax.ppermute(whole_sum(theirs, helped_theirs), 'ctx', pairs)  7.09 us
  transfers between devices with their start and end apart: 5, of which 2 were waited for; matrix products, arithmetic and copies ran while one was open for 10% of the time, Pallas kernels for 0%

profile of v4, /device:TPU:0, one launch (start us, length us, event | category | flops | bytes accessed | tf_op | source)
XLA Modules:
  0.0 279.7 jit_solution(8902486415213723689)
XLA Ops:
  0.0 0.0 copy-start
  0.0 0.0 copy-start.1
  0.0 1.7 fusion.33
  1.7 0.0 copy-done
  1.8 0.0 copy-done.1
  1.8 0.3 maximum_bitcast_fusion
  2.0 1.8 pad_maximum_fusion.wgt
  3.9 1.7 broadcast_in_dim.33.zeros
  5.5 199.8 %shard_map.55 = (bf16[512,8192]{1,0:T(8,128)(2,1)}, bf16[512,8192]{1,0:T(8,128)(2,1)}, bf16[8192,640]{1,0:T(8,128)(2,1)}, bf16[512,2048]{1,0:T(8,128)(2,1)}, bf16[512,2048]{1,0:T(8,128)(2,1)}) custom-call(bf16[512,2048]{1,0:T(8,128)(2,1)} %tok.1, bf16[2,1024,640]{2,1,0:T(8,128)(2,1)} %pad_maximum_fusion.wgt, bf16[2048,640]{1,0:T(8,128)(2,1)} %broadcast_in_dim.33.zeros), custom_call_target="tpu_custom_call" | custom-call | tf_op jit(solution)/shard_map/pallas_call | solution.py:214
  205.4 0.0 copy-start.2
  205.4 5.2 %fusion.11 = bf16[512,640]{1,0:T(8,128)(2,1)} fusion(bf16[512,2048]{1,0:T(8,128)(2,1)} %get-tuple-element.16, bf16[8192,640]{1,0:T(8,128)(2,1)} %get-tuple-element.15, s32[]{:T(128)S(6)} %select_n.43), kind=kOutput, calls=%fused_computation.15 | convolution fusion | flops 1342504960 | bytes 5373956 | tf_op jit(solution)/shard_map/dot_general | solution.py:245
  210.5 1.3 collective-permute-start
  211.8 0.0 slice-start
  211.8 4.3 %fusion.14 = bf16[512,640]{1,0:T(8,128)(2,1)S(1)} fusion(bf16[512,2048]{1,0:T(8,128)(2,1)} %get-tuple-element.20, bf16[8192,640]{1,0:T(8,128)(2,1)} %get-tuple-element.15, s32[]{:T(128)S(6)} %select_n.43), kind=kOutput, calls=%fused_computation.16 | convolution fusion | flops 1342504960 | bytes 5373956 | tf_op jit(solution)/shard_map/dot_general | solution.py:245
  216.1 1.5 collective-permute-start.1
  217.6 0.0 copy-done.2
  217.6 0.0 slice-start.1
  217.6 9.4 %fusion.36 = f32[512,640]{1,0:T(8,128)S(1)} fusion(bf16[512,8192]{1,0:T(8,128)(2,1)} %get-tuple-element.19, bf16[8192,640]{1,0:T(8,128)(2,1)S(1)} %copy-done.2), kind=kOutput, calls=%fused_computation.48 | convolution fusion | flops 5368709120 | bytes 20185088 | tf_op jit(solution)/shard_map/dot_general | solution.py:245
  227.0 16.7 %collective-permute-done.1 = bf16[512,640]{1,0:T(8,128)(2,1)S(1)} collective-permute-done((bf16[512,640]{1,0:T(8,128)(2,1)S(1)}, bf16[512,640]{1,0:T(8,128)(2,1)S(1)}, u32[]{:S(2)}, u32[]{:S(2)}) %collective-permute-start.1) | collective-permute-done | bytes 655392 | tf_op jit(solution)/shard_map/ppermute | solution.py:248
  243.7 0.1 add_convert_fusion
  243.8 1.6 collective-permute-start.2
  245.4 0.0 slice-done
  245.4 0.0 slice-done.1
  245.4 6.7 %fusion.35 = f32[512,640]{1,0:T(8,128)S(1)} fusion(bf16[512,8192]{1,0:T(8,128)(2,1)S(1)} %bitcast.56, bf16[8192,640]{1,0:T(8,128)(2,1)S(1)} %copy-done.2), kind=kOutput, calls=%fused_computation.47 | convolution fusion | flops 5368709120 | bytes 20185088 | tf_op jit(solution)/shard_map/dot_general | solution.py:245
  252.1 0.8 fusion.34
  253.0 0.0 collective-permute-done
  253.0 7.1 %collective-permute-done.2 = bf16[512,640]{1,0:T(8,128)(2,1)S(1)} collective-permute-done((bf16[512,640]{1,0:T(8,128)(2,1)S(1)}, bf16[512,640]{1,0:T(8,128)(2,1)S(1)}, u32[]{:S(2)}, u32[]{:S(2)}) %collective-permute-start.2) | collective-permute-done | bytes 655392 | tf_op jit(solution)/shard_map/ppermute | solution.py:255
  260.1 0.3 broadcast_select_fusion.1
  260.4 3.4 %collective-permute-start.3 = (bf16[512,128]{1,0:T(8,128)(2,1)S(1)}, bf16[512,128]{1,0:T(8,128)(2,1)S(1)}, u32[]{:S(2)}, u32[]{:S(2)}) collective-permute-start(bf16[512,128]{1,0:T(8,128)(2,1)S(1)} %slice.24), channel_id=1, source_target_pairs={{0,4},{4,8},{8,12},{12,16},{16,20},{20,24},{24,28},{1,5},{5,9},{9,... | collective-permute-start | bytes 393224 | tf_op jit(solution)/shard_map/ppermute | solution.py:16
  263.8 1.0 compare_and_fusion
  264.9 2.1 collective-permute-start.4
  267.0 0.0 collective-permute-done.3
  267.1 2.9 %fusion = (f32[8,512]{1,0:T(8,128)S(1)}, f32[1024,512,8]{1,0,2:T(8,128)S(1)}) fusion(pred[512,1024]{0,1:T(8,128)(4,1)S(1)} %compare_and_fusion, bf16[512,128]{1,0:T(8,128)(2,1)S(1)} %slice.24, bf16[512,128]{1,0:T(8,128)(2,1)S(1)} %collective-permute-done.3, bf16[512,512]{1,0:T(8,128)(2,1)S(1)} %slice.26, bf16[512,512]{1,0:T(8,128)(2,1)S(1)} %slice.25), kind=kOutput, calls=%fused_computation.2 | convolution fusion | flops 1088942080 | bytes 18628608 | tf_op jit(solution)/shard_map/thgd,shd->hgts/dot_general | solution.py:21
  269.9 4.0 %fusion.1 = f32[8,512]{1,0:T(8,128)S(1)} fusion(f32[1024,512,8]{1,0,2:T(8,128)S(1)} %get-tuple-element.30, f32[8,512]{1,0:T(8,128)S(1)} %get-tuple-element.29, pred[512,1024]{0,1:T(8,128)(4,1)S(1)} %compare_and_fusion), kind=kLoop, calls=%fused_computation.3 | loop fusion | flops 20967424 | bytes 17334272 | tf_op jit(solution)/shard_map/reduce_sum | solution.py:27
  274.0 0.0 collective-permute-done.4
  274.0 4.3 %divide_convert_fusion = bf16[8,512,128]{1,2,0:T(8,128)(2,1)S(1)} fusion(f32[8,512]{1,0:T(8,128)S(1)} %fusion.1, f32[1024,512,8]{1,0,2:T(8,128)S(1)} %get-tuple-element.30, f32[8,512]{1,0:T(8,128)S(1)} %get-tuple-element.29, pred[512,1024]{0,1:T(8,128)(4,1)S(1)} %compare_and_fusion, bf16[512,128]{1,0:T(8,128)(2,1)S(1)} %slice.27, ...), kind=kOutput, calls=%fused_computation.13 | convolution fusion | flops 1096286208 | bytes 18644992 | tf_op jit(solution)/shard_map/hgts,shd->hgtd/dot_general | solution.py:29
  278.3 1.3 copy.9
  (8 shorter events, 0.1 us)
Async XLA Ops:
  0.0 1.7 copy-start
  0.0 1.8 copy-start.1
  205.4 12.3 %copy-start.2 = (bf16[8192,640]{1,0:T(8,128)(2,1)S(1)}, bf16[8192,640]{1,0:T(8,128)(2,1)}, u32[]{:S(2)}) copy-start(bf16[8192,640]{1,0:T(8,128)(2,1)} %get-tuple-element.15) | copy-start | bytes 31457284
  210.5 42.5 %collective-permute-start = (bf16[512,640]{1,0:T(8,128)(2,1)}, bf16[512,640]{1,0:T(8,128)(2,1)S(1)}, u32[]{:S(2)}, u32[]{:S(2)}) collective-permute-start(bf16[512,640]{1,0:T(8,128)(2,1)} %fusion.11), channel_id=1, source_target_pairs={{8,0},{12,4},{16,24},{20,28},{9,1},{13,5},{17,25},{21,29},{10,2},{... | collective-permute-start | bytes 1966088 | tf_op jit(solution)/shard_map/ppermute | solution.py:248
  211.8 33.6 %slice-start = ((s8[8388608]{0:T(1024)(128)(4,1)}), s8[4194304]{0:T(1024)(128)(4,1)S(1)}, s32[]{:S(2)}) async-start(s8[8388608]{0:T(1024)(128)(4,1)} %bitcast.55), calls=%async_computation | async-start | bytes 8388608
  216.1 27.5 %collective-permute-start.1 = (bf16[512,640]{1,0:T(8,128)(2,1)S(1)}, bf16[512,640]{1,0:T(8,128)(2,1)S(1)}, u32[]{:S(2)}, u32[]{:S(2)}) collective-permute-start(bf16[512,640]{1,0:T(8,128)(2,1)S(1)} %fusion.14), channel_id=1, source_target_pairs={{8,0},{12,4},{16,24},{20,28},{9,1},{13,5},{17,25},{21,29},{10,2},{... | collective-permute-start | bytes 1966088 | tf_op jit(solution)/shard_map/ppermute | solution.py:248
  217.6 27.8 %slice-start.1 = ((s8[8388608]{0:T(1024)(128)(4,1)}), s8[4194304]{0:T(1024)(128)(4,1)S(1)}, s32[]{:S(2)}) async-start(s8[8388608]{0:T(1024)(128)(4,1)} %bitcast.55), calls=%async_computation.1 | async-start | bytes 8388608
  243.8 16.3 %collective-permute-start.2 = (bf16[512,640]{1,0:T(8,128)(2,1)S(1)}, bf16[512,640]{1,0:T(8,128)(2,1)S(1)}, u32[]{:S(2)}, u32[]{:S(2)}) collective-permute-start(bf16[512,640]{1,0:T(8,128)(2,1)S(1)} %add_convert_fusion), channel_id=1, source_target_pairs={{0,4},{4,0},{8,12},{12,8},{16,20},{20,16},{24,28},{28,24},{1,5},{5... | collective-permute-start | bytes 1966088 | tf_op jit(solution)/shard_map/ppermute | solution.py:255
  260.4 6.7 %collective-permute-start.3 = (bf16[512,128]{1,0:T(8,128)(2,1)S(1)}, bf16[512,128]{1,0:T(8,128)(2,1)S(1)}, u32[]{:S(2)}, u32[]{:S(2)}) collective-permute-start(bf16[512,128]{1,0:T(8,128)(2,1)S(1)} %slice.24), channel_id=1, source_target_pairs={{0,4},{4,8},{8,12},{12,16},{16,20},{20,24},{24,28},{1,5},{5,9},{9,... | collective-permute-start | bytes 393224 | tf_op jit(solution)/shard_map/ppermute | solution.py:16
  264.9 9.1 %collective-permute-start.4 = (bf16[512,128]{1,0:T(8,128)(2,1)S(1)}, bf16[512,128]{1,0:T(8,128)(2,1)S(1)}, u32[]{:S(2)}, u32[]{:S(2)}) collective-permute-start(bf16[512,128]{1,0:T(8,128)(2,1)S(1)} %slice.27), channel_id=1, source_target_pairs={{0,4},{4,8},{8,12},{12,16},{16,20},{20,24},{24,28},{1,5},{5,9},{9,... | collective-permute-start | bytes 393224 | tf_op jit(solution)/shard_map/ppermute | solution.py:16

commit v5 on v4

--- a/solution.py
+++ b/solution.py
@@ -101,12 +101,13 @@
     their_core = copy(columns(theirs, kv), columns(theirs, kv), ts.at[5], tr.at[5], core)
     last_core = copy(columns(theirs, other_chip), columns(theirs, other_chip), ts.at[6], tr.at[6], core)
 
+    own_across.start()
+    own_far.start()
+    own_core.start()
+    for p in range(pieces):
+        both_ways(0, 0, p)
     for p in range(pieces):
         y_copy(p).start()
-        both_ways(0, 0, p)
-    own_far.start()
-    own_across.start()
-    own_core.start()
     edge, inner = (z == 0) | (z == lines - 1), (z == 1) | (z == lines - 2)
     core_index, strip = kv % 2, tok.shape[0] // 2
     opposite = (lines - 1) * (1 - jnp.minimum(z, 1))
@@ -126,10 +127,6 @@
                  wgt.at[y], wgt_all.at[pl.ds(pl.multiple_of(ctx * depth, depth), depth), :], loc.at[1])]
     for c in local:
         c.start()
-    for p in range(pieces):
-        y_copy(p).wait_recv()
-        both_ways(0, 1, p)
-
     def relay_mine():
         own_far.wait_recv()
         mine_core.start()
@@ -151,25 +148,31 @@
             ext_across.start()
             ext_core.start()
 
-    relays = {(1, 0): relay_mine, (1, 1): relay_theirs, (2, 0): relay_ext}
+    def travel(d, s):
+        for p in range(pieces):
+            @pl.when(z >= d)
+            def _(p=p):
+                up_copy(d - 1, s, p).wait_recv()
+                if d < lines - 2:
+                    pl.when(has_up)(lambda: up_copy(d, s, p).start())
+
+            @pl.when(z + d < lines)
+            def _(p=p):
+                down_copy(d - 1, s, p).wait_recv()
+                if d < lines - 2:
+                    pl.when(has_down)(lambda: down_copy(d, s, p).start())
+
+    travel(1, 0)
+    relay_mine()
+    relay_theirs()
+    for p in range(pieces):
+        y_copy(p).wait_recv()
+        both_ways(0, 1, p)
+    for d in range(2, lines - 1):
+        travel(d, 0)
+    relay_ext()
     for d in range(1, lines - 1):
-        for s in range(2):
-            for p in range(pieces):
-                @pl.when(z >= d)
-                def _(d=d, s=s, p=p):
-                    up_copy(d - 1, s, p).wait_recv()
-                    if d < lines - 2:
-                        pl.when(has_up)(lambda: up_copy(d, s, p).start())
-
-                @pl.when(z + d < lines)
-                def _(d=d, s=s, p=p):
-                    down_copy(d - 1, s, p).wait_recv()
-                    if d < lines - 2:
-                        pl.when(has_down)(lambda: down_copy(d, s, p).start())
-            if (d, s) in relays:
-                relays.pop((d, s))()
-    for key in sorted(relays):
-        relays[key]()
+        travel(d, 1)
 
     their_far.wait_recv()
     last_core.start()
@@ -247,13 +250,17 @@
     def help_end(ext):
         return lax.ppermute(project(ext, opposite).astype(jnp.bfloat16), "ctx", inward)
 
-    def whole_sum(whole, helped):
-        own, helped = lax.optimization_barrier((project(whole, weights), helped))
+    def finish(own, helped):
         return (own + helped.astype(jnp.float32)).astype(jnp.bfloat16)
 
-    helped_theirs, helped_mine = help_end(ext_theirs), help_end(ext_mine)
-    received = lax.ppermute(whole_sum(theirs, helped_theirs), "ctx", pairs)
-    kept = whole_sum(mine, helped_mine)
+    helped_theirs = help_end(ext_theirs)
+    own_theirs, ext_mine = lax.optimization_barrier((project(theirs, weights), ext_mine))
+    own_theirs, helped_theirs = lax.optimization_barrier((own_theirs, helped_theirs))
+    received = lax.ppermute(finish(own_theirs, helped_theirs), "ctx", pairs)
+    helped_mine = help_end(ext_mine)
+    own_mine, helped_mine, received = lax.optimization_barrier(
+        (project(mine, weights), helped_mine, received))
+    kept = finish(own_mine, helped_mine)
     first_side = lax.axis_index("ctx") % 2 == 0
     low = jnp.where(first_side, kept, received)
     high = jnp.where(first_side, received, kept)

time: 280 us -> 285 us (1.018)
  waiting for transfers between devices: 23.8 us -> 10.3 us
  Pallas kernels: 200 us -> 213 us
  matrix products: 32.8 us -> 36 us
    pallas_call x1, Pallas kernels: 200 us -> 213 us  [gathered(): pl.pallas_call(functools.partial(gather_kernel, lines, pieces), out_shape...]
    ppermute x1, waiting for transfers between devices: 7.09 us -> 0.01 us  [shards(): received = lax.ppermute(finish(own_theirs, helped_theirs), 'ctx', pairs)]
    ppermute x2, waiting for transfers between devices: 16.7 us -> 10.2 us  [help_end(): lax.ppermute(project(ext, opposite).astype(jnp.bfloat16), 'ctx', inward)]
    dot_general x4, matrix products: 25.5 us -> 28.7 us  [project(): return jnp.dot(whole, matrix, preferred_element_type=jnp.float32)]
  transfers between devices with their start and end apart: 5 -> 5, of which waited for: 2 -> 2; matrix products, arithmetic and copies ran while one was open for 10% -> 12% of each run, Pallas kernels for 0% -> 0%
where the time goes in v5:
time: 285 us
  Pallas kernels  213 us (75%)
  matrix products  36 us (13%)
  starting transfers between devices  11.8 us (4%)
  waiting for transfers between devices  10.3 us (4%)
  other arithmetic  7.52 us (3%)
  local copies, waits for them, and re-layouts  5.7 us (2%)
    pallas_call x1, Pallas kernels, gathered(): pl.pallas_call(functools.partial(gather_kernel, lines, pieces), out_shape...  213 us
    dot_general x4, matrix products, project(): return jnp.dot(whole, matrix, preferred_element_type=jnp.float32)  28.7 us
    ppermute x2, waiting for transfers between devices, help_end(): lax.ppermute(project(ext, opposite).astype(jnp.bfloat16), 'ctx', inward)  10.2 us
    ppermute x2, starting transfers between devices, shifted(): return lax.ppermute(shard, axis, pairs)  7.48 us
  transfers between devices with their start and end apart: 5, of which 2 were waited for; matrix products, arithmetic and copies ran while one was open for 12% of the time, Pallas kernels for 0%

profile of v5, /device:TPU:0, one launch (start us, length us, event | category | flops | bytes accessed | tf_op | source)
XLA Modules:
  0.0 284.7 jit_solution(4319290885786924169)
XLA Ops:
  0.0 0.0 copy-start
  0.0 0.0 copy-start.1
  0.0 1.7 fusion.33
  1.7 0.0 copy-done
  1.8 0.0 copy-done.1
  1.8 0.3 maximum_bitcast_fusion
  2.0 1.8 pad_maximum_fusion.wgt
  3.9 1.7 broadcast_in_dim.33.zeros
  5.6 213.1 %shard_map.55 = (bf16[512,8192]{1,0:T(8,128)(2,1)}, bf16[512,8192]{1,0:T(8,128)(2,1)}, bf16[8192,640]{1,0:T(8,128)(2,1)}, bf16[512,2048]{1,0:T(8,128)(2,1)}, bf16[512,2048]{1,0:T(8,128)(2,1)}) custom-call(bf16[512,2048]{1,0:T(8,128)(2,1)} %tok.1, bf16[2,1024,640]{2,1,0:T(8,128)(2,1)} %pad_maximum_fusion.wgt, bf16[2048,640]{1,0:T(8,128)(2,1)} %broadcast_in_dim.33.zeros), custom_call_target="tpu_custom_call" | custom-call | tf_op jit(solution)/shard_map/pallas_call | solution.py:217
  218.7 0.0 slice-start
  218.7 0.0 slice-start.3
  218.7 4.3 %fusion.14 = bf16[512,640]{1,0:T(8,128)(2,1)S(1)} fusion(bf16[512,2048]{1,0:T(8,128)(2,1)} %get-tuple-element.23, bf16[8192,640]{1,0:T(8,128)(2,1)} %get-tuple-element.18, s32[]{:T(128)S(6)} %select_n.43), kind=kOutput, calls=%fused_computation.16 | convolution fusion | flops 1342504960 | bytes 5373956 | tf_op jit(solution)/shard_map/dot_general | solution.py:248
  223.0 1.3 collective-permute-start.1
  224.3 0.0 slice-start.1
  224.3 0.0 slice-start.2
  224.4 0.0 copy-start.2
  224.4 0.0 slice-start.4
  224.4 15.1 %fusion.36 = f32[512,640]{1,0:T(8,128)S(1)} fusion(bf16[512,8192]{1,0:T(8,128)(2,1)} %get-tuple-element.19, bf16[8192,640]{1,0:T(8,128)(2,1)} %get-tuple-element.18), kind=kOutput, calls=%fused_computation.48 | convolution fusion | flops 5368709120 | bytes 20185088 | tf_op jit(solution)/shard_map/dot_general | solution.py:248
  239.5 0.0 slice-done
  239.5 0.0 slice-done.1
  239.5 0.0 slice-done.2
  239.5 0.0 copy-done.2
  239.6 2.6 fusion.11
  242.2 1.5 collective-permute-start
  243.7 0.1 collective-permute-done.1
  243.8 0.1 add_convert_fusion.1
  243.9 1.6 collective-permute-start.2
  245.5 0.0 slice-done.3
  245.5 0.0 slice-done.4
  245.5 6.7 %fusion.35 = f32[512,640]{1,0:T(8,128)S(1)} fusion(bf16[512,8192]{1,0:T(8,128)(2,1)S(1)} %bitcast.58, bf16[8192,640]{1,0:T(8,128)(2,1)S(1)} %bitcast.56), kind=kOutput, calls=%fused_computation.47 | convolution fusion | flops 5368709120 | bytes 20185088 | tf_op jit(solution)/shard_map/dot_general | solution.py:248
  252.2 0.8 fusion.34
  253.0 10.1 %collective-permute-done = bf16[512,640]{1,0:T(8,128)(2,1)S(1)} collective-permute-done((bf16[512,640]{1,0:T(8,128)(2,1)}, bf16[512,640]{1,0:T(8,128)(2,1)S(1)}, u32[]{:S(2)}, u32[]{:S(2)}) %collective-permute-start) | collective-permute-done | bytes 655392 | tf_op jit(solution)/shard_map/ppermute | solution.py:251
  263.2 0.0 collective-permute-done.2
  263.2 0.3 broadcast_select_fusion.1
  263.5 3.4 %collective-permute-start.3 = (bf16[512,128]{1,0:T(8,128)(2,1)S(1)}, bf16[512,128]{1,0:T(8,128)(2,1)S(1)}, u32[]{:S(2)}, u32[]{:S(2)}) collective-permute-start(bf16[512,128]{1,0:T(8,128)(2,1)S(1)} %slice.24), channel_id=1, source_target_pairs={{0,4},{4,8},{8,12},{12,16},{16,20},{20,24},{24,28},{1,5},{5,9},{9,... | collective-permute-start | bytes 393224 | tf_op jit(solution)/shard_map/ppermute | solution.py:16
  266.9 1.0 compare_and_fusion
  268.0 4.1 %collective-permute-start.4 = (bf16[512,128]{1,0:T(8,128)(2,1)S(1)}, bf16[512,128]{1,0:T(8,128)(2,1)S(1)}, u32[]{:S(2)}, u32[]{:S(2)}) collective-permute-start(bf16[512,128]{1,0:T(8,128)(2,1)S(1)} %slice.27), channel_id=1, source_target_pairs={{0,4},{4,8},{8,12},{12,16},{16,20},{20,24},{24,28},{1,5},{5,9},{9,... | collective-permute-start | bytes 393224 | tf_op jit(solution)/shard_map/ppermute | solution.py:16
  272.0 0.0 collective-permute-done.3
  272.1 2.9 %fusion = (f32[8,512]{1,0:T(8,128)S(1)}, f32[1024,512,8]{1,0,2:T(8,128)S(1)}) fusion(pred[512,1024]{0,1:T(8,128)(4,1)S(1)} %compare_and_fusion, bf16[512,128]{1,0:T(8,128)(2,1)S(1)} %slice.24, bf16[512,128]{1,0:T(8,128)(2,1)S(1)} %collective-permute-done.3, bf16[512,512]{1,0:T(8,128)(2,1)S(1)} %slice.26, bf16[512,512]{1,0:T(8,128)(2,1)S(1)} %slice.25), kind=kOutput, calls=%fused_computation.2 | convolution fusion | flops 1088942080 | bytes 18628608 | tf_op jit(solution)/shard_map/thgd,shd->hgts/dot_general | solution.py:21
  274.9 4.0 %fusion.1 = f32[8,512]{1,0:T(8,128)S(1)} fusion(f32[1024,512,8]{1,0,2:T(8,128)S(1)} %get-tuple-element.36, f32[8,512]{1,0:T(8,128)S(1)} %get-tuple-element.35, pred[512,1024]{0,1:T(8,128)(4,1)S(1)} %compare_and_fusion), kind=kLoop, calls=%fused_computation.3 | loop fusion | flops 20967424 | bytes 17334272 | tf_op jit(solution)/shard_map/reduce_sum | solution.py:27
  279.0 0.0 collective-permute-done.4
  279.0 4.3 %divide_convert_fusion = bf16[8,512,128]{1,2,0:T(8,128)(2,1)S(1)} fusion(f32[8,512]{1,0:T(8,128)S(1)} %fusion.1, f32[1024,512,8]{1,0,2:T(8,128)S(1)} %get-tuple-element.36, f32[8,512]{1,0:T(8,128)S(1)} %get-tuple-element.35, pred[512,1024]{0,1:T(8,128)(4,1)S(1)} %compare_and_fusion, bf16[512,128]{1,0:T(8,128)(2,1)S(1)} %slice.27, ...), kind=kOutput, calls=%fused_computation.13 | convolution fusion | flops 1096286208 | bytes 18644992 | tf_op jit(solution)/shard_map/hgts,shd->hgtd/dot_general | solution.py:29
  283.3 1.3 copy.9
  (9 shorter events, 0.1 us)
Async XLA Ops:
  0.0 1.7 copy-start
  0.0 1.8 copy-start.1
  218.7 20.8 %slice-start = ((s8[10485760]{0:T(1024)(128)(4,1)}), s8[4194304]{0:T(1024)(128)(4,1)S(1)}, s32[]{:S(2)}) async-start(s8[10485760]{0:T(1024)(128)(4,1)} %bitcast.55), calls=%async_computation | async-start | bytes 8388608
  218.7 26.8 %slice-start.3 = ((s8[8388608]{0:T(1024)(128)(4,1)}), s8[4194304]{0:T(1024)(128)(4,1)S(1)}, s32[]{:S(2)}) async-start(s8[8388608]{0:T(1024)(128)(4,1)} %bitcast.57), calls=%async_computation.3 | async-start | bytes 8388608
  223.0 20.7 %collective-permute-start.1 = (bf16[512,640]{1,0:T(8,128)(2,1)S(1)}, bf16[512,640]{1,0:T(8,128)(2,1)S(1)}, u32[]{:S(2)}, u32[]{:S(2)}) collective-permute-start(bf16[512,640]{1,0:T(8,128)(2,1)S(1)} %fusion.14), channel_id=1, source_target_pairs={{8,0},{12,4},{16,24},{20,28},{9,1},{13,5},{17,25},{21,29},{10,2},{... | collective-permute-start | bytes 1966088 | tf_op jit(solution)/shard_map/ppermute | solution.py:251
  224.3 15.2 %slice-start.1 = ((s8[10485760]{0:T(1024)(128)(4,1)}), s8[4194304]{0:T(1024)(128)(4,1)S(1)}, s32[]{:S(2)}) async-start(s8[10485760]{0:T(1024)(128)(4,1)} %bitcast.55), calls=%async_computation.1 | async-start | bytes 8388608
  224.3 15.2 %slice-start.2 = ((s8[10485760]{0:T(1024)(128)(4,1)}), s8[2097152]{0:T(1024)(128)(4,1)S(1)}, s32[]{:S(2)}) async-start(s8[10485760]{0:T(1024)(128)(4,1)} %bitcast.55), calls=%async_computation.2 | async-start | bytes 4194304
  224.4 15.2 %copy-start.2 = (bf16[512,2048]{1,0:T(8,128)(2,1)S(1)}, bf16[512,2048]{1,0:T(8,128)(2,1)}, u32[]{:S(2)}) copy-start(bf16[512,2048]{1,0:T(8,128)(2,1)} %get-tuple-element.21) | copy-start | bytes 6291460
  224.4 21.1 %slice-start.4 = ((s8[8388608]{0:T(1024)(128)(4,1)}), s8[4194304]{0:T(1024)(128)(4,1)S(1)}, s32[]{:S(2)}) async-start(s8[8388608]{0:T(1024)(128)(4,1)} %bitcast.57), calls=%async_computation.4 | async-start | bytes 8388608
  242.2 21.0 %collective-permute-start = (bf16[512,640]{1,0:T(8,128)(2,1)}, bf16[512,640]{1,0:T(8,128)(2,1)S(1)}, u32[]{:S(2)}, u32[]{:S(2)}) collective-permute-start(bf16[512,640]{1,0:T(8,128)(2,1)} %fusion.11), channel_id=1, source_target_pairs={{8,0},{12,4},{16,24},{20,28},{9,1},{13,5},{17,25},{21,29},{10,2},{... | collective-permute-start | bytes 1966088 | tf_op jit(solution)/shard_map/ppermute | solution.py:251
  243.9 19.3 %collective-permute-start.2 = (bf16[512,640]{1,0:T(8,128)(2,1)S(1)}, bf16[512,640]{1,0:T(8,128)(2,1)S(1)}, u32[]{:S(2)}, u32[]{:S(2)}) collective-permute-start(bf16[512,640]{1,0:T(8,128)(2,1)S(1)} %add_convert_fusion.1), channel_id=1, source_target_pairs={{0,4},{4,0},{8,12},{12,8},{16,20},{20,16},{24,28},{28,24},{1,5},{5... | collective-permute-start | bytes 1966088 | tf_op jit(solution)/shard_map/ppermute | solution.py:259
  263.5 8.6 %collective-permute-start.3 = (bf16[512,128]{1,0:T(8,128)(2,1)S(1)}, bf16[512,128]{1,0:T(8,128)(2,1)S(1)}, u32[]{:S(2)}, u32[]{:S(2)}) collective-permute-start(bf16[512,128]{1,0:T(8,128)(2,1)S(1)} %slice.24), channel_id=1, source_target_pairs={{0,4},{4,8},{8,12},{12,16},{16,20},{20,24},{24,28},{1,5},{5,9},{9,... | collective-permute-start | bytes 393224 | tf_op jit(solution)/shard_map/ppermute | solution.py:16
  268.0 11.0 %collective-permute-start.4 = (bf16[512,128]{1,0:T(8,128)(2,1)S(1)}, bf16[512,128]{1,0:T(8,128)(2,1)S(1)}, u32[]{:S(2)}, u32[]{:S(2)}) collective-permute-start(bf16[512,128]{1,0:T(8,128)(2,1)S(1)} %slice.27), channel_id=1, source_target_pairs={{0,4},{4,8},{8,12},{12,16},{16,20},{20,24},{24,28},{1,5},{5,9},{9,... | collective-permute-start | bytes 393224 | tf_op jit(solution)/shard_map/ppermute | solution.py:16

commit v6 on v3

--- a/solution.py
+++ b/solution.py
@@ -43,7 +43,7 @@
     other_core, other_chip = (kv // 2) * 2 + (1 - kv % 2), (1 - kv // 2) * 2 + kv % 2
     core, far = {"kv": other_core}, {"kv": other_chip}
     has_up, has_down = z < lines - 1, z > 0
-    height, depth = tok.shape[1], wgt.shape[1]
+    height, depth, width = tok.shape[1], wgt.shape[0], wgt_all.shape[1]
     rows = depth // pieces
 
     barrier = pltpu.get_barrier_semaphore()
@@ -70,7 +70,7 @@
         return wgt_all.at[pl.ds(start, rows), :]
 
     def own(half, p):
-        return wgt.at[half, pl.ds(p * rows, rows), :]
+        return wgt.at[pl.ds(p * rows, rows), pl.ds(pl.multiple_of(half * width, width), width)]
 
     def block(off, s, p):
         return own(y, p) if (off, s) == (0, 0) else place(z + off, y if s == 0 else 1 - y, p)
@@ -109,7 +109,8 @@
     own_core.start()
     local = [pltpu.make_async_copy(tok, columns(mine, kv), loc.at[0]),
              pltpu.make_async_copy(
-                 wgt.at[y], wgt_all.at[pl.ds(pl.multiple_of(ctx * depth, depth), depth), :], loc.at[1])]
+                 wgt.at[:, pl.ds(pl.multiple_of(y * width, width), width)],
+                 wgt_all.at[pl.ds(pl.multiple_of(ctx * depth, depth), depth), :], loc.at[1])]
     for c in local:
         c.start()
     for p in range(pieces):
@@ -166,7 +167,7 @@
 
 def gathered(tokens, weights):
     lines = lax.axis_size("ctx") // 2
-    _, depth, width = weights.shape
+    depth, width = weights.shape[0], weights.shape[1] // 2
     pieces = max(1, depth // 256)
     dma = pltpu.SemaphoreType.DMA
     line_sems = [dma((lines, 2, pieces))] * 4
@@ -189,10 +190,8 @@
 def shards(tokens, segment_ids, query_weight, key_weight, value_projection_matrix):
     rows = tokens.shape[0]
     wide, half = key_weight.shape[1], query_weight.shape[1] // 2
-    packed = jnp.stack([
-        jnp.concatenate([key_weight, query_weight[:, :half]], axis=1),
-        jnp.concatenate([value_projection_matrix, query_weight[:, half:]], axis=1),
-    ])
+    packed = jnp.concatenate(
+        [key_weight, query_weight[:, :half], value_projection_matrix, query_weight[:, half:]], axis=1)
     mine, theirs, weights = gathered(tokens, packed)
 
     def project(whole):
@@ -206,7 +205,8 @@
     high = jnp.where(first_side, received, kept)
     key_rows, value_rows = low[:, :wide], high[:, :wide]
     query_rows = jnp.concatenate([low[:, wide:], high[:, wide:]], axis=1)
-    prev_key, prev_value = shifted((key_rows, value_rows), "ctx", 1)
+    previous = shifted(jnp.concatenate([key_rows, value_rows], axis=1), "ctx", 1)
+    prev_key, prev_value = previous[:, :wide], previous[:, wide:]
     kv_heads = key_weight.shape[1] // HEAD_DIMENSION
     query_group = query_weight.shape[1] // (HEAD_DIMENSION * kv_heads)
     query_matrix = query_rows.reshape(rows, kv_heads, query_group, HEAD_DIMENSION)

time: 228 us -> 228 us (level)
    another operation x2 -> x0, other arithmetic: 3.13 us -> none  [shards(): jnp.stack([jnp.concatenate([key_weight, query_weight[:, :half]], axis=1),...]
    concatenate x0 -> x2, other arithmetic: none -> 2.65 us  [the longest x1 2.61 us: shards(): jnp.concatenate([key_weight, query_weight[:, :half], value_projection_mat...]
    ppermute x2 -> x1, starting transfers between devices: 5.53 us -> 3.62 us  [shifted(): return lax.ppermute(shard, axis, pairs)]
  transfers between devices with their start and end apart: 3 -> 2, of which waited for: 2 -> 2; matrix products, arithmetic and copies ran while one was open for 7% -> 4% of each run, Pallas kernels for 0% -> 0%
where the time goes in v6:
time: 228 us
  Pallas kernels  175 us (77%)
  matrix products  26.1 us (11%)
  waiting for transfers between devices  9.13 us (4%)
  other arithmetic  7.79 us (3%)
  starting transfers between devices  5.2 us (2%)
  local copies, waits for them, and re-layouts  3.96 us (2%)
    pallas_call x1, Pallas kernels, gathered(): pl.pallas_call(functools.partial(gather_kernel, lines, pieces), out_shape...  175 us
    dot_general x2, matrix products, project(): jnp.dot(whole, weights, preferred_element_type=jnp.float32)  18.9 us
    ppermute x1, waiting for transfers between devices, shards(): received = lax.ppermute(project(theirs), 'ctx', pairs)  6.52 us
  transfers between devices with their start and end apart: 2, of which 2 were waited for; matrix products, arithmetic and copies ran while one was open for 4% of the time, Pallas kernels for 0%

profile of v6, /device:TPU:0, one launch (start us, length us, event | category | flops | bytes accessed | tf_op | source)
XLA Modules:
  0.0 227.7 jit_solution(11098645110600513760)
XLA Ops:
  0.0 1.7 fusion.21
  1.7 2.6 %pad_maximum_fusion.wgt = bf16[1024,1280]{1,0:T(8,128)(2,1)} fusion(bf16[1024,512]{1,0:T(8,128)(2,1)S(1)} %get-tuple-element.16, bf16[1024,128]{1,0:T(8,128)(2,1)} %param.9, bf16[1024,512]{1,0:T(8,128)(2,1)S(1)} %get-tuple-element.15, bf16[1024,128]{1,0:T(8,128)(2,1)} %param.8), kind=kLoop, calls=%fused_computation.8 | loop fusion | flops 10485760 | bytes 5242880 | tf_op jit(solution)/shard_map/concatenate | solution.py:193
  4.3 175.3 %shard_map.55 = (bf16[512,8192]{1,0:T(8,128)(2,1)}, bf16[512,8192]{1,0:T(8,128)(2,1)}, bf16[8192,640]{1,0:T(8,128)(2,1)}) custom-call(bf16[512,2048]{1,0:T(8,128)(2,1)} %tok.1, bf16[1024,1280]{1,0:T(8,128)(2,1)} %pad_maximum_fusion.wgt), custom_call_target="tpu_custom_call" | custom-call | tf_op jit(solution)/shard_map/pallas_call | solution.py:176
  179.6 0.0 copy-start
  179.6 0.0 copy-start.1
  179.6 12.3 %convolution_convert_fusion = bf16[512,640]{1,0:T(8,128)(2,1)S(1)} fusion(bf16[512,8192]{1,0:T(8,128)(2,1)} %get-tuple-element.12, bf16[8192,640]{1,0:T(8,128)(2,1)} %get-tuple-element.11), kind=kOutput, calls=%fused_computation.11 | convolution fusion | flops 5369036800 | bytes 19529728 | tf_op jit(solution)/shard_map/dot_general | solution.py:198
  191.9 1.6 collective-permute-start
  193.5 0.0 copy-done
  193.5 0.0 copy-done.1
  193.5 6.7 %convolution_convert_fusion.1 = bf16[512,640]{1,0:T(8,128)(2,1)S(1)} fusion(bf16[512,8192]{1,0:T(8,128)(2,1)S(1)} %copy-done.1, bf16[8192,640]{1,0:T(8,128)(2,1)S(1)} %copy-done), kind=kOutput, calls=%fused_computation.12 | convolution fusion | flops 5369036800 | bytes 19529728 | tf_op jit(solution)/shard_map/dot_general | solution.py:198
  200.2 0.8 fusion.23
  201.0 6.5 %collective-permute-done = bf16[512,640]{1,0:T(8,128)(2,1)S(1)} collective-permute-done((bf16[512,640]{1,0:T(8,128)(2,1)S(1)}, bf16[512,640]{1,0:T(8,128)(2,1)S(1)}, u32[]{:S(2)}, u32[]{:S(2)}) %collective-permute-start) | collective-permute-done | bytes 655392 | tf_op jit(solution)/shard_map/ppermute | solution.py:201
  207.6 0.1 broadcast_select_fusion.1
  207.8 3.6 %collective-permute-start.1 = (bf16[512,256]{1,0:T(8,128)(2,1)S(1)}, bf16[512,256]{1,0:T(8,128)(2,1)S(1)}, u32[]{:S(2)}, u32[]{:S(2)}) collective-permute-start(bf16[512,256]{1,0:T(8,128)(2,1)S(1)} %pad_maximum_fusion.1), channel_id=1, source_target_pairs={{0,4},{4,8},{8,12},{12,16},{16,20},{20,24},{24,28},{1,5},{5,9},{9,... | collective-permute-start | bytes 786440 | tf_op jit(solution)/shard_map/ppermute | solution.py:16
  211.4 1.0 compare_and_fusion
  212.5 2.6 %collective-permute-done.1 = bf16[512,256]{1,0:T(8,128)(2,1)S(1)} collective-permute-done((bf16[512,256]{1,0:T(8,128)(2,1)S(1)}, bf16[512,256]{1,0:T(8,128)(2,1)S(1)}, u32[]{:S(2)}, u32[]{:S(2)}) %collective-permute-start.1) | collective-permute-done | bytes 262176 | tf_op jit(solution)/shard_map/ppermute | solution.py:16
  215.1 2.9 %fusion = (f32[8,512]{1,0:T(8,128)S(1)}, f32[1024,512,8]{1,0,2:T(8,128)S(1)}) fusion(pred[512,1024]{0,1:T(8,128)(4,1)S(1)} %compare_and_fusion, bf16[512,128]{1,0:T(8,128)(2,1)S(1)} %slice.32, bf16[512,128]{1,0:T(8,128)(2,1)S(1)} %get-tuple-element.20, bf16[512,512]{1,0:T(8,128)(2,1)S(1)} %slice.36, bf16[512,512]{1,0:T(8,128)(2,1)S(1)} %slice.35), kind=kOutput, calls=%fused_computation.2 | convolution fusion | flops 1088942080 | bytes 18628608 | tf_op jit(solution)/shard_map/thgd,shd->hgts/dot_general | solution.py:21
  218.0 4.0 %fusion.1 = f32[8,512]{1,0:T(8,128)S(1)} fusion(f32[1024,512,8]{1,0,2:T(8,128)S(1)} %get-tuple-element.24, f32[8,512]{1,0:T(8,128)S(1)} %get-tuple-element.23, pred[512,1024]{0,1:T(8,128)(4,1)S(1)} %compare_and_fusion), kind=kLoop, calls=%fused_computation.3 | loop fusion | flops 20967424 | bytes 17334272 | tf_op jit(solution)/shard_map/reduce_sum | solution.py:27
  222.0 4.3 %divide_convert_fusion = bf16[8,512,128]{1,2,0:T(8,128)(2,1)S(1)} fusion(f32[8,512]{1,0:T(8,128)S(1)} %fusion.1, f32[1024,512,8]{1,0,2:T(8,128)S(1)} %get-tuple-element.24, f32[8,512]{1,0:T(8,128)S(1)} %get-tuple-element.23, pred[512,1024]{0,1:T(8,128)(4,1)S(1)} %compare_and_fusion, bf16[512,128]{1,0:T(8,128)(2,1)S(1)} %slice.33, ...), kind=kOutput, calls=%fused_computation.9 | convolution fusion | flops 1096286208 | bytes 18644992 | tf_op jit(solution)/shard_map/hgts,shd->hgtd/dot_general | solution.py:29
  226.4 1.3 copy.9
  (9 shorter events, 0.2 us)
Async XLA Ops:
  179.6 13.9 %copy-start = (bf16[8192,640]{1,0:T(8,128)(2,1)S(1)}, bf16[8192,640]{1,0:T(8,128)(2,1)}, u32[]{:S(2)}) copy-start(bf16[8192,640]{1,0:T(8,128)(2,1)} %get-tuple-element.11) | copy-start | bytes 31457284
  179.6 13.9 %copy-start.1 = (bf16[512,8192]{1,0:T(8,128)(2,1)S(1)}, bf16[512,8192]{1,0:T(8,128)(2,1)}, u32[]{:S(2)}) copy-start(bf16[512,8192]{1,0:T(8,128)(2,1)} %get-tuple-element.10) | copy-start | bytes 25165828
  191.9 15.7 %collective-permute-start = (bf16[512,640]{1,0:T(8,128)(2,1)S(1)}, bf16[512,640]{1,0:T(8,128)(2,1)S(1)}, u32[]{:S(2)}, u32[]{:S(2)}) collective-permute-start(bf16[512,640]{1,0:T(8,128)(2,1)S(1)} %convolution_convert_fusion), channel_id=1, source_target_pairs={{0,4},{4,0},{8,12},{12,8},{16,20},{20,16},{24,28},{28,24},{1,5},{5... | collective-permute-start | bytes 1966088 | tf_op jit(solution)/shard_map/ppermute | solution.py:201
  207.8 7.3 %collective-permute-start.1 = (bf16[512,256]{1,0:T(8,128)(2,1)S(1)}, bf16[512,256]{1,0:T(8,128)(2,1)S(1)}, u32[]{:S(2)}, u32[]{:S(2)}) collective-permute-start(bf16[512,256]{1,0:T(8,128)(2,1)S(1)} %pad_maximum_fusion.1), channel_id=1, source_target_pairs={{0,4},{4,8},{8,12},{12,16},{16,20},{20,24},{24,28},{1,5},{5,9},{9,... | collective-permute-start | bytes 786440 | tf_op jit(solution)/shard_map/ppermute | solution.py:16
